TPU v7x, 128 devices: a whole 4x4x4 slice. The times are simulated.
128 devices in a mesh: dp: 32 (over x, z, core), mp: 4 (over y).
Axes of the slice: x: 4, y: 4, z: 4, core: 2. Of those that a mesh axis runs over, the one named last changes fastest.
Arguments:
- block_states: bfloat16 [64, 128, 4096], P('dp', None, 'mp'), may hold values from -6 to 6
- norm_gain: bfloat16 [4096], P('mp'), may hold values from 0.099609375 to 1.8984375
- key_weight: bfloat16 [4096, 4096], P(None, 'mp'), may hold values from -0.09375 to 0.09375
- value_weight: bfloat16 [4096, 4096], P(None, 'mp'), may hold values from -0.09375 to 0.09375
- queries: bfloat16 [8192, 4096], P('dp', 'mp'), may hold values from -21 to 21
- wanted: int32 [32, 32], replicated, may hold values from -1 to 1, as said below
Outputs:
- attended: bfloat16 [8192, 4096], P('dp', 'mp')
Inputs may be any that keep to these rules, and one draw needn't show every extreme that they name: `wanted`: each question reads from between 8 and 24 encoder indices, at most one block from each; some question reads from exactly 24.
All inputs are finite; a program needn't handle non-finite values.
Results may differ from a plain program's by a relative error of at most 0.0065.
The roundings to bfloat16 on the way count: a program that leaves them out, or rounds other values in their place, can miss the bound.
Values may be sent and summed in bfloat16 or wider, within the bound.
No kernel may reach another device: no remote copies, remote signals or barrier semaphores. Data moves between devices by JAX's collectives and lax.ppermute only.
A program may use at most 128 MiB of HBM per device.

v0:
```python
import math

import jax
import jax.numpy as jnp
from jax import lax
from jax.sharding import PartitionSpec as P

HD = 64


def attend(running, query_heads, blocks, usable):
    top_old, total_old, summed = running
    head_count = query_heads.shape[1]
    cols = head_count * HD
    key_count = blocks.shape[0] * blocks.shape[1]
    key_part = blocks[:, :, :cols].reshape(key_count, head_count, HD)
    value_part = blocks[:, :, cols:].reshape(key_count, head_count, HD)
    scores = jnp.einsum("qhd,khd->hqk", query_heads, key_part, preferred_element_type=jnp.float32)
    live_keys = jnp.repeat(usable, blocks.shape[1])[None, None, :]
    scores = jnp.where(live_keys, scores, -1e30)
    top_new = jnp.maximum(top_old, jnp.max(scores, axis=-1))
    weights = jnp.where(live_keys, jnp.exp(scores - top_new[:, :, None]), 0.0).astype(jnp.bfloat16)
    factor = jnp.exp(top_old - top_new)
    total_new = total_old * factor + jnp.sum(weights.astype(jnp.float32), axis=-1)
    summed = summed * factor[:, :, None] + jnp.einsum(
        "hqk,khd->hqd", weights, value_part, preferred_element_type=jnp.float32
    )
    return (top_new, total_new, summed)


def sweep_blocks(running, query_heads, blocks, usable):
    nblocks = blocks.shape[0]
    group_size = math.gcd(nblocks, max(1, 512 // blocks.shape[1]))
    shaped = blocks.reshape(nblocks // group_size, group_size, blocks.shape[1], blocks.shape[2])
    usable_groups = usable.reshape(nblocks // group_size, group_size)

    def scan_step(state_now, item_pair):
        return (attend(state_now, query_heads, item_pair[0], item_pair[1]), None)

    running, _ = lax.scan(scan_step, running, (shaped, usable_groups))
    return running


def local(block_states, norm_gain, key_weight, value_weight, queries, wanted):
    gathered, gain_full = (
        lax.all_gather(block_states, "mp", axis=2, tiled=True),
        lax.all_gather(norm_gain, "mp", axis=0, tiled=True),
    )
    floats = gathered.astype(jnp.float32)
    mean_square = jnp.mean(floats * floats, axis=-1, keepdims=True)
    normed = (floats * lax.rsqrt(mean_square + 1e-06) * gain_full.astype(jnp.float32)).astype(
        jnp.bfloat16
    )
    per_device = normed.shape[0]
    flat_rows = normed.reshape(per_device * normed.shape[1], normed.shape[2])
    key_rows = jnp.dot(flat_rows, key_weight, preferred_element_type=jnp.float32).astype(
        jnp.bfloat16
    )
    value_rows = jnp.dot(flat_rows, value_weight, preferred_element_type=jnp.float32).astype(
        jnp.bfloat16
    )
    kv_pairs = jnp.concatenate([key_rows, value_rows], axis=-1).reshape(
        per_device, normed.shape[1], 2 * key_rows.shape[1]
    )
    my_index = lax.axis_index("dp")
    wanted_row = lax.dynamic_index_in_dim(wanted, my_index, 0, keepdims=False)
    head_count = queries.shape[1] // HD
    query_heads = queries.reshape(queries.shape[0], head_count, HD)
    start_state = (
        jnp.full((head_count, queries.shape[0]), -1e30, jnp.float32),
        jnp.zeros((head_count, queries.shape[0]), jnp.float32),
        jnp.zeros((head_count, queries.shape[0], HD), jnp.float32),
    )
    piece_kv = lax.all_gather(kv_pairs, "dp", axis=0, tiled=True)
    block_index = jnp.arange(piece_kv.shape[0], dtype=jnp.int32)
    owner = block_index // per_device
    local_index = block_index % per_device
    usable = jnp.take(wanted_row, owner) == local_index
    final_state = sweep_blocks(start_state, query_heads, piece_kv, usable)
    summed = final_state[2] / final_state[1][:, :, None]
    return (
        summed.transpose(1, 0, 2).reshape(queries.shape[0], queries.shape[1]).astype(jnp.bfloat16)
    )


def solution(mesh):
    return jax.shard_map(
        local,
        mesh=mesh,
        in_specs=(P("dp", None, "mp"), P("mp"), P(None, "mp"), P(None, "mp"), P("dp", "mp"), P()),
        out_specs=P("dp", "mp"),
        check_vma=False,
    )
```

profile of v0, /device:TPU:1, one launch (start us, length us, event | category | flops | bytes accessed | tf_op | source)
XLA Modules:
  0.0 467.8 jit_solution(8861269419751338692)
XLA Ops:
  7.3 9.6 %all_gather.10 = bf16[4096]{0:T(1024)(128)(2,1)S(1)} all-gather(bf16[1024]{0:T(1024)(128)(2,1)} %param.9), channel_id=1, replica_groups=mesh['dp'=32,'mp'=4] {'mp'}, dimensions={0}, use_global_device_ids=true | all-gather | bytes 10240 | tf_op jit(solution)/shard_map/all_gather | solution.py:47
  16.9 26.2 %all-gather.3.cloned.1.call-done = bf16[2,128,4096]{2,1,0:T(8,128)(2,1)} async-done(((bf16[2,128,1024]{2,1,0:T(8,128)(2,1)}), bf16[2,128,4096]{2,1,0:T(8,128)(2,1)}) %all-gather.3.cloned.1.call-update) | async-done | bytes 2097168 | tf_op jit(solution)/shard_map/all_gather | solution.py:46
  47.7 5.9 %convolution_convert_fusion = bf16[256,1024]{1,0:T(8,128)(2,1)S(1)} fusion(bf16[256,4096]{1,0:T(8,128)(2,1)S(1)} %bitcast.58, bf16[4096,1024]{1,0:T(8,128)(2,1)} %param.11), kind=kOutput, calls=%fused_computation.21 | convolution fusion | flops 2147745792 | bytes 11010048 | tf_op jit(solution)/shard_map/dot_general | solution.py:59
  59.2 112.5 %all-gather.5.cloned.1.call-done = bf16[64,128,2048]{2,1,0:T(8,128)(2,1)} async-done(((bf16[2,128,2048]{2,1,0:T(8,128)(2,1)}), bf16[64,128,2048]{2,1,0:T(8,128)(2,1)}) %all-gather.5.cloned.1.call-update) | async-done | bytes 33554448 | tf_op jit(solution)/shard_map/all_gather | solution.py:74
  171.7 286.8 %while.15 = (s32[]{:T(128)}, f32[16,256]{1,0:T(8,128)S(1)}, f32[16,256]{1,0:T(8,128)S(1)}, f32[16,256,64]{1,2,0:T(8,128)}, pred[16,4]{1,0:T(8,128)(4,1)S(1)}, /*...) while((s32[]{:T(128)}, f32[16,256]{1,0:T(8,128)S(1)}, ...), condition=%wide.region_4.5_spmd.clone, body=%wide.region_1.4_spmd.clone.sunk | while | flops 554455040 | bytes 46909056 | solution.py:40
  171.8 3.2 constant_dynamic-slice_fusion.2
  188.6 3.2 constant_dynamic-slice_fusion.2
  206.6 3.2 constant_dynamic-slice_fusion.2
  224.6 3.2 constant_dynamic-slice_fusion.2
  242.6 3.2 constant_dynamic-slice_fusion.2
  260.6 3.2 constant_dynamic-slice_fusion.2
  278.6 3.2 constant_dynamic-slice_fusion.2
  281.8 3.1 copy.21
  296.6 3.2 constant_dynamic-slice_fusion.2
  299.8 3.1 copy.21
  314.6 3.2 constant_dynamic-slice_fusion.2
  332.6 3.2 constant_dynamic-slice_fusion.2
  350.6 3.2 constant_dynamic-slice_fusion.2
  368.6 3.2 constant_dynamic-slice_fusion.2
  371.8 3.1 copy.21
  386.6 3.2 constant_dynamic-slice_fusion.2
  404.6 3.2 constant_dynamic-slice_fusion.2
  422.6 3.2 constant_dynamic-slice_fusion.2
  440.6 3.2 constant_dynamic-slice_fusion.2
  (222 shorter events, 238.6 us)
Async XLA Ops:
  6.5 50.7 %copy-start = (s32[32,32]{1,0:T(8,128)S(1)}, s32[32,32]{1,0:T(8,128)}, u32[]{:S(2)}) copy-start(s32[32,32]{1,0:T(8,128)} %param.13) | copy-start | bytes 12292
  6.5 36.6 %all-gather.3.cloned.1.call-start = ((), (), s32[]{:S(2)}) async-start(), calls=%async_computation | async-start | bytes 2621440 | tf_op jit(solution)/shard_map/all_gather | solution.py:46
  7.3 164.5 %all-gather.5.cloned.1.call-start = ((), (), s32[]{:S(2)}) async-start(), calls=%async_computation.1 | async-start | bytes 34603008 | tf_op jit(solution)/shard_map/all_gather | solution.py:74
  45.2 8.4 %slice-start = ((s8[8388608]{0:T(1024)(128)(4,1)}), s8[4194304]{0:T(1024)(128)(4,1)S(1)}, s32[]{:S(2)}) async-start(s8[8388608]{0:T(1024)(128)(4,1)} %bitcast.61), calls=%async_computation.2 | async-start | bytes 8388608
  47.7 6.0 %slice-start.1 = ((s8[8388608]{0:T(1024)(128)(4,1)}), s8[4194304]{0:T(1024)(128)(4,1)S(1)}, s32[]{:S(2)}) async-start(s8[8388608]{0:T(1024)(128)(4,1)} %bitcast.61), calls=%async_computation.3 | async-start | bytes 8388608
  53.7 4.5 copy-start.2
  458.6 2.3 copy-start.1
Sparse Core Ops, SparseCore 0:
  9.0 34.0 all-gather.2
  57.3 114.3 all-gather.4
where the time goes:
time: 471 us; the launch traced here: 468 us
  local copies, waits for them, and re-layouts  163 us (35%)
  waiting for transfers between devices  140 us (30%)
  matrix products  97.2 us (21%)
  other arithmetic  44.3 us (9%)
  between operations  13.6 us (3%)
  blocking collectives  9.56 us (2%)
    all_gather x1, waiting for transfers between devices, local(): piece_kv = lax.all_gather(kv_pairs, 'dp', axis=0, tiled=True)  113 us
    dynamic_slice x32, local copies, waits for them, and re-layouts, sweep_blocks(): running, _ = lax.scan(scan_step, running, (shaped, usable_groups))  100 us
    dot_general x16, matrix products, attend(): jnp.einsum('hqk,khd->hqd', weights, value_part, preferred_element_type=jn...  46.9 us
    dot_general x16, matrix products, attend(): jnp.einsum('qhd,khd->hqk', query_heads, key_part, preferred_element_type=...  42 us
    reduce_sum x16, other arithmetic, attend(): jnp.sum(weights.astype(jnp.float32), axis=-1)  36.9 us
    slice x16, local copies, waits for them, and re-layouts, attend(): value_part = blocks[:, :, cols:].reshape(key_count, head_count, HD)  27.3 us
    all_gather x1, waiting for transfers between devices, local(): lax.all_gather(block_states, 'mp', axis=2, tiled=True)  26.2 us
    reshape x16, local copies, waits for them, and re-layouts, attend(): key_part = blocks[:, :, :cols].reshape(key_count, head_count, HD)  23.4 us
  transfers between devices with their start and end apart: 2, of which 2 were waited for; matrix products, arithmetic and copies ran while one was open for 0% of the time, Pallas kernels for 0%

commit v1 on v0

v1 whole, which is shorter than its diff:
```python
import functools

import jax
import jax.numpy as jnp
from jax import lax
from jax.experimental import pallas as pl
from jax.experimental.pallas import tpu as pltpu
from jax.sharding import PartitionSpec as P

AXES = ("dp", "mp")
SIDE = 4
HD = 64
BLOCK = 128
HALF = 512
PAIRS = 4
TILE = 128
QTOK = 256
STAT = 32
OFFSETS = (0, 3, 1, 2)
F32, BF16 = jnp.float32, jnp.bfloat16


def device_id(x, y, z, c):
    return ((x * SIDE + z) * 2 + c) * SIDE + y


def permutation(move):
    pairs = []
    for x in range(SIDE):
        for z in range(SIDE):
            for c in range(2):
                for y in range(SIDE):
                    pairs.append((device_id(x, y, z, c), device_id(*move(x, y, z, c))))
    return pairs


def along_y(step):
    return permutation(lambda x, y, z, c: (x, (y + step) % SIDE, z, c))


def along_ring(step, first_along_x):
    def move(x, y, z, c):
        if (c == 0) == first_along_x:
            return ((x + step) % SIDE, y, z, c)
        return (x, y, (z + step) % SIDE, c)

    return permutation(move)


CORE_SWAP = permutation(lambda x, y, z, c: (x, y, z, 1 - c))


def send(array, pairs):
    return lax.ppermute(array, AXES, pairs)


def gather(array, ring):
    return [array] + [send(array, ring(step)) for step in (1, -1, 2)]


def place():
    index = lax.axis_index("dp")
    return index >> 3, (index >> 1) & 3, index & 1


def project_kernel(*refs):
    x_refs, g_refs = refs[0:4], refs[4:8]
    key_hbm, value_hbm = refs[8:10]
    mine_ref, away_ref = refs[10:12]
    normed, weights, sems = refs[12:]
    rows = x_refs[0].shape[0]
    width = x_refs[0].shape[1]
    y = lax.axis_index("mp")
    core = place()[2]
    copies = []
    for slot in range(4):
        first = pl.multiple_of(((y + OFFSETS[slot]) & 3) * width, width)
        for which, hbm in enumerate((key_hbm, value_hbm)):
            copy = pltpu.make_async_copy(
                hbm.at[pl.ds(first, width), :], weights.at[which, slot], sems.at[which, slot]
            )
            copy.start()
            copies.append(copy)
    total = jnp.zeros((rows, 1), F32)
    for x_ref in x_refs:
        floats = x_ref[...].astype(F32)
        total += jnp.sum(floats * floats, axis=-1, keepdims=True)
    scale = lax.rsqrt(total * (1.0 / (4 * width)) + 1e-06)
    for slot in range(4):
        floats = x_refs[slot][...].astype(F32)
        normed[slot] = (floats * scale * g_refs[slot][...].astype(F32)).astype(BF16)
    for copy in copies:
        copy.wait()
    for half, out_ref in enumerate((mine_ref, away_ref)):
        first = pl.multiple_of((core ^ half) * HALF, HALF)
        for which in range(2):
            product = jnp.zeros((rows, HALF), F32)
            for slot in range(4):
                product += jnp.dot(
                    normed[slot],
                    weights[which, slot, :, pl.ds(first, HALF)],
                    preferred_element_type=F32,
                )
            for pair in range(PAIRS):
                for block in range(rows // BLOCK):
                    part = product[
                        block * BLOCK : (block + 1) * BLOCK, pair * TILE : (pair + 1) * TILE
                    ]
                    if which == 1:
                        part = part.T
                    out_ref[block, which, pair] = part.astype(BF16)


def project(states, gains, key_weight, value_weight):
    rows, width = states[0].shape
    blocks = rows // BLOCK
    shape = jax.ShapeDtypeStruct((blocks, 2, PAIRS, TILE, BLOCK), BF16)
    vmem = pl.BlockSpec(memory_space=pltpu.VMEM)
    hbm = pl.BlockSpec(memory_space=pl.ANY)
    return pl.pallas_call(
        project_kernel,
        out_shape=(shape, shape),
        in_specs=[vmem] * 8 + [hbm] * 2,
        out_specs=(vmem, vmem),
        scratch_shapes=[
            pltpu.VMEM((4, rows, width), BF16),
            pltpu.VMEM((2, 4, width, 2 * HALF), BF16),
            pltpu.SemaphoreType.DMA((2, 4)),
        ],
        compiler_params=pltpu.CompilerParams(vmem_limit_bytes=40 * 2**20),
        cost_estimate=pl.CostEstimate(
            flops=2 * rows * 4 * width * 4 * HALF, bytes_accessed=18 * 2**20, transcendentals=0
        ),
        name="project",
    )(*states, *gains, key_weight, value_weight)


def attend_kernel(*refs):
    wanted = refs[0]
    q_hbm, kv_hbm, out_hbm = refs[1:5], refs[5:9], refs[9:13]
    qbuf, kvbuf, masked, scores, sums, outbuf, chosen, in_sems, out_sems = refs[13:]
    x, z, core = place()
    copies = []
    for slot in range(4):
        copy = pltpu.make_async_copy(
            q_hbm[slot], qbuf.at[pl.ds(2 * slot, 2)], in_sems.at[0, slot]
        )
        copy.start()
        copies.append(copy)
        copy = pltpu.make_async_copy(
            kv_hbm[slot], kvbuf.at[pl.ds(2 * slot, 2)], in_sems.at[1, slot]
        )
        copy.start()
        copies.append(copy)
    for copy in copies:
        copy.wait()

    def dp_index(along_x, offset, swapped):
        ex = jnp.where(along_x, (x + offset) & 3, x)
        ez = jnp.where(along_x, z, (z + offset) & 3)
        return (ex * 4 + ez) * 2 + (core ^ swapped)

    lane_half = lax.broadcasted_iota(jnp.int32, (QTOK, TILE), 1) // HD
    row = lax.broadcasted_iota(jnp.int32, (16, 2 * BLOCK), 0) // 8
    col = lax.broadcasted_iota(jnp.int32, (16, 2 * BLOCK), 1) // BLOCK
    ones = jnp.where(row == col, 1.0, 0.0).astype(BF16)
    empty = jnp.zeros((HD, BLOCK), BF16)

    def question(index, carry):
        slot = index >> 1
        offset = jnp.where(slot == 0, 0, jnp.where(slot == 1, 3, jnp.where(slot == 2, 1, 2)))
        q_index = dp_index(core == 1, offset, index & 1)
        count = jnp.int32(0)
        for t in range(4):
            for swapped in range(2):
                local = wanted[q_index, dp_index(core == 0, OFFSETS[t], swapped)]
                chosen[count] = (t * 2 + swapped) * 2 + jnp.maximum(local, 0)
                count = count + jnp.where(local >= 0, 1, 0)
        for pair in range(PAIRS):
            part = qbuf[index, :, pair * TILE : (pair + 1) * TILE]
            for head in range(2):
                masked[pair, head] = jnp.where(lane_half == head, part, jnp.zeros_like(part))

        def score(step, tops):
            place_of = chosen[step]
            out = []
            for pair in range(PAIRS):
                keys = kvbuf[place_of >> 1, place_of & 1, 0, pair]
                for head in range(2):
                    s = lax.dot_general(
                        keys,
                        masked[pair, head],
                        (((1,), (1,)), ((), ())),
                        preferred_element_type=F32,
                    )
                    scores[step, pair, head] = s
                    top = jnp.max(s.reshape(BLOCK // 8, 8, QTOK), axis=0)
                    out.append(jnp.maximum(tops[2 * pair + head], top))
            return tuple(out)

        low = jnp.full((8, QTOK), -1e30, F32)
        tops = lax.fori_loop(0, count, score, (low,) * (2 * PAIRS))
        tops = [jnp.max(top, axis=0, keepdims=True) for top in tops]
        sums[...] = jnp.zeros_like(sums)

        def weigh(step, carry):
            place_of = chosen[step]
            for pair in range(PAIRS):
                probs = [
                    jnp.exp(scores[step, pair, head] - tops[2 * pair + head]).astype(BF16)
                    for head in range(2)
                ]
                values = kvbuf[place_of >> 1, place_of & 1, 1, pair]
                left = jnp.concatenate(
                    [
                        jnp.concatenate([values[:HD], empty], axis=1),
                        jnp.concatenate([empty, values[HD:]], axis=1),
                        ones,
                    ],
                    axis=0,
                )
                sums[pair] += jnp.dot(
                    left, jnp.concatenate(probs, axis=0), preferred_element_type=F32
                )
            return carry

        lax.fori_loop(0, count, weigh, 0)
        stats = []
        for pair in range(PAIRS):
            for head in range(2):
                total = sums[pair, TILE + 8 * head : TILE + 8 * head + 1, :]
                some = total > 0.0
                part = sums[pair, head * HD : (head + 1) * HD, :]
                part = part * (1.0 / jnp.where(some, total, 1.0))
                first = pair * TILE + head * HD
                outbuf[index, first : first + HD, :] = part.astype(BF16)
                top = tops[2 * pair + head]
                stats.append(jnp.where(some, top + jnp.log(jnp.where(some, total, 1.0)), -1e30))
        rest = jnp.concatenate(stats, axis=0)
        parts = []
        for _ in range(3):
            part = rest.astype(BF16).astype(F32)
            parts.append(part)
            rest = rest - part
        parts.append(jnp.zeros_like(rest))
        outbuf[index, HALF : HALF + STAT, :] = jnp.concatenate(parts, axis=0).astype(BF16)
        return carry

    lax.fori_loop(0, 8, question, 0)
    copies = []
    for slot in range(4):
        copy = pltpu.make_async_copy(
            outbuf.at[pl.ds(2 * slot, 2)], out_hbm[slot], out_sems.at[slot]
        )
        copy.start()
        copies.append(copy)
    for copy in copies:
        copy.wait()


def attend(wanted, queries, blocks):
    hbm = pl.BlockSpec(memory_space=pl.ANY)
    shape = jax.ShapeDtypeStruct((2, HALF + STAT, QTOK), BF16)
    return pl.pallas_call(
        attend_kernel,
        out_shape=(shape,) * 4,
        in_specs=[pl.BlockSpec(memory_space=pltpu.SMEM)] + [hbm] * 8,
        out_specs=(hbm,) * 4,
        scratch_shapes=[
            pltpu.VMEM((8, QTOK, HALF), BF16),
            pltpu.VMEM((8, 2, 2, PAIRS, TILE, BLOCK), BF16),
            pltpu.VMEM((PAIRS, 2, QTOK, TILE), BF16),
            pltpu.VMEM((8, PAIRS, 2, BLOCK, QTOK), F32),
            pltpu.VMEM((PAIRS, TILE + 16, QTOK), F32),
            pltpu.VMEM((8, HALF + STAT, QTOK), BF16),
            pltpu.SMEM((16,), jnp.int32),
            pltpu.SemaphoreType.DMA((2, 4)),
            pltpu.SemaphoreType.DMA((4,)),
        ],
        compiler_params=pltpu.CompilerParams(vmem_limit_bytes=40 * 2**20),
        name="attend",
    )(wanted, *queries, *blocks)


def merged(refs, which):
    stats = []
    for ref in refs:
        stat = ref[which, HALF : HALF + STAT, :].astype(F32)
        stats.append(stat[0:8] + stat[8:16] + stat[16:24])
    top = functools.reduce(jnp.maximum, stats)
    weights = [jnp.exp(stat - top) for stat in stats]
    inverse = 1.0 / sum(weights)
    weights = [weight * inverse for weight in weights]
    heads = []
    for head in range(2 * PAIRS):
        heads.append(
            sum(
                ref[which, head * HD : (head + 1) * HD, :].astype(F32) * weight[head : head + 1]
                for ref, weight in zip(refs, weights)
            )
        )
    return jnp.concatenate(heads, axis=0)


def merge_away_kernel(a, b, c, d, out_ref):
    out_ref[...] = merged((a, b, c, d), 1).T.astype(BF16)


def merge_home_kernel(a, b, c, d, other_ref, out_ref):
    core = place()[2]
    mine = pl.multiple_of(core * HALF, HALF)
    away = pl.multiple_of((1 - core) * HALF, HALF)
    out_ref[:, pl.ds(mine, HALF)] = merged((a, b, c, d), 0).T.astype(BF16)
    out_ref[:, pl.ds(away, HALF)] = other_ref[...]


def merge(partials):
    vmem = pl.BlockSpec(memory_space=pltpu.VMEM)
    away = pl.pallas_call(
        merge_away_kernel,
        out_shape=jax.ShapeDtypeStruct((QTOK, HALF), BF16),
        in_specs=[vmem] * 4,
        out_specs=vmem,
        name="merge_away",
    )(*partials)
    other = send(away, CORE_SWAP)
    return pl.pallas_call(
        merge_home_kernel,
        out_shape=jax.ShapeDtypeStruct((QTOK, 2 * HALF), BF16),
        in_specs=[vmem] * 5,
        out_specs=vmem,
        name="merge_home",
    )(*partials, other)


def both_cores(mine, away):
    return jnp.concatenate([mine, send(away, CORE_SWAP)], axis=0)


def local(block_states, norm_gain, key_weight, value_weight, queries, wanted):
    core = place()[2]
    states = gather(block_states.reshape(2 * BLOCK, -1), along_y)
    gains = gather(norm_gain.reshape(1, -1), along_y)
    mine = lax.dynamic_slice_in_dim(queries, core * HALF, HALF, 1)
    away = lax.dynamic_slice_in_dim(queries, (1 - core) * HALF, HALF, 1)
    kv_ring = functools.partial(along_ring, first_along_x=True)
    q_ring = functools.partial(along_ring, first_along_x=False)
    slots_q = gather(both_cores(mine[None], away[None]), q_ring)
    mine, away = project(states, gains, key_weight, value_weight)
    slots_kv = gather(both_cores(mine[None], away[None]), kv_ring)
    partials = attend(wanted, slots_q, slots_kv)
    returned = [partials[0]] + [
        send(partial, q_ring(-step)) for partial, step in zip(partials[1:], (1, -1, 2))
    ]
    return merge(returned)


def solution(mesh):
    return jax.shard_map(
        local,
        mesh=mesh,
        in_specs=(P("dp", None, "mp"), P("mp"), P(None, "mp"), P(None, "mp"), P("dp", "mp"), P()),
        out_specs=P("dp", "mp"),
        check_vma=False,
    )
```

time: 471 us -> 145 us (0.31)
  local copies, waits for them, and re-layouts: 163 us -> 7.65 us
  matrix products: 97.2 us -> 0 us
  waiting for transfers between devices: 140 us -> 67.7 us
  other arithmetic: 44.3 us -> 0.15 us
  Pallas kernels: 0 us -> 37.7 us
  starting transfers between devices: 0.04 us -> 32.5 us
  between operations: 13.6 us -> 0.08 us
  blocking collectives: 9.56 us -> 0 us
    all_gather x2 -> x0, waiting for transfers between devices: 139 us -> none  [the longest x1 113 us: local(): piece_kv = lax.all_gather(kv_pairs, 'dp', axis=0, tiled=True)]
    dynamic_slice x32 -> x0, local copies, waits for them, and re-layouts: 100 us -> none  [sweep_blocks(): running, _ = lax.scan(scan_step, running, (shaped, usable_groups))]
    dot_general x34 -> x0, matrix products: 97.2 us -> none  [the longest x16 46.9 us: attend(): jnp.einsum('hqk,khd->hqd', weights, value_part, preferred_element_type=jn...]
    ppermute x0 -> x18, waiting for transfers between devices: none -> 67.7 us  [send(): return lax.ppermute(array, AXES, pairs)]
    reduce_sum x17 -> x0, other arithmetic: 39 us -> none  [the longest x16 36.9 us: attend(): jnp.sum(weights.astype(jnp.float32), axis=-1)]
    pallas_call x0 -> x4, Pallas kernels: none -> 37.7 us  [the longest x1 23.8 us: attend(): pl.pallas_call(attend_kernel, out_shape=(shape,) * 4, in_specs=[pl.BlockS...]
    ppermute x0 -> x18, starting transfers between devices: none -> 32.5 us  [send(): return lax.ppermute(array, AXES, pairs)]
    reshape x32 -> x1, local copies, waits for them, and re-layouts: 30.5 us -> 0.69 us  [local(): gains = gather(norm_gain.reshape(1, -1), along_y)]
  transfers between devices with their start and end apart: 2 -> 18, of which waited for: 2 -> 10; matrix products, arithmetic and copies ran while one was open for 0% -> 1% of each run, Pallas kernels for 0% -> 0%
where the time goes in v1:
time: 145 us; the launch traced here: 146 us
  waiting for transfers between devices  67.7 us (47%)
  Pallas kernels  37.7 us (26%)
  starting transfers between devices  32.5 us (22%)
  local copies, waits for them, and re-layouts  7.65 us (5%)
    ppermute x18, waiting for transfers between devices, send(): return lax.ppermute(array, AXES, pairs)  67.7 us
    ppermute x18, starting transfers between devices, send(): return lax.ppermute(array, AXES, pairs)  32.5 us
    pallas_call x1, Pallas kernels, attend(): pl.pallas_call(attend_kernel, out_shape=(shape,) * 4, in_specs=[pl.BlockS...  23.8 us
    pallas_call x1, Pallas kernels, project(): pl.pallas_call(project_kernel, out_shape=(shape, shape), in_specs=[vmem]...  8.59 us
    unnamed x18, local copies, waits for them, and re-layouts  6.93 us
  transfers between devices with their start and end apart: 18, of which 10 were waited for; matrix products, arithmetic and copies ran while one was open for 1% of the time, Pallas kernels for 0%

profile of v1, /device:TPU:1, one launch (start us, length us, event | category | flops | bytes accessed | tf_op | source)
XLA Modules:
  0.0 145.8 jit_solution(9780785725920374839)
XLA Ops:
  0.0 3.7 %collective-permute-start.6 = (bf16[256,1024]{1,0:T(8,128)(2,1)}, bf16[256,1024]{1,0:T(8,128)(2,1)S(1)}, u32[]{:S(2)}, u32[]{:S(2)}) collective-permute-start(bf16[256,1024]{1,0:T(8,128)(2,1)} %bitcast.7), channel_id=1, source_target_pairs={{0,2},{1,3},{2,0},{3,1},{4,6},{5,7},{6,4},{7,5},{8,10},{9,11},{10,... | collective-permute-start | bytes 1572872 | tf_op jit(solution)/shard_map/ppermute | solution.py:54
  6.6 2.1 %collective-permute-start.8 = (bf16[1,1024]{1,0:T(2,128)(2,1)S(1)}, bf16[1,1024]{1,0:T(2,128)(2,1)S(1)}, u32[]{:S(2)}, u32[]{:S(2)}) collective-permute-start(bf16[1,1024]{1,0:T(2,128)(2,1)S(1)} %reshape.7.refs_4_), channel_id=1, source_target_pairs={{0,3},{1,0},{2,1},{3,2},{4,7},{5,4},{6,5},{7,6},{8,11},{9,8},{10,9... | collective-permute-start | bytes 6152 | tf_op jit(solution)/shard_map/ppermute | solution.py:54
  8.7 17.7 %collective-permute-done.9.refs_7_ = bf16[1,1024]{1,0:T(2,128)(2,1)S(1)} collective-permute-done((bf16[1,1024]{1,0:T(2,128)(2,1)S(1)}, bf16[1,1024]{1,0:T(2,128)(2,1)S(1)}, u32[]{:S(2)}, u32[]{:S(2)}) %collective-permute-start.9) | collective-permute-done | bytes 2080 | tf_op jit(solution)/shard_map/ppermute | solution.py:54
  26.4 1.3 collective-permute-start.7
  27.7 2.4 %collective-permute-done.7.refs_5_ = bf16[1,1024]{1,0:T(2,128)(2,1)S(1)} collective-permute-done((bf16[1,1024]{1,0:T(2,128)(2,1)S(1)}, bf16[1,1024]{1,0:T(2,128)(2,1)S(1)}, u32[]{:S(2)}, u32[]{:S(2)}) %collective-permute-start.7) | collective-permute-done | bytes 2080 | tf_op jit(solution)/shard_map/ppermute | solution.py:54
  30.2 3.4 %copy-done = bf16[4096,1024]{1,0:T(8,128)(2,1)S(1)} copy-done((bf16[4096,1024]{1,0:T(8,128)(2,1)S(1)}, bf16[4096,1024]{1,0:T(8,128)(2,1)}, u32[]{:S(2)}) %copy-start) | copy-done | bytes 8388632
  33.5 1.0 copy-done.2
  34.6 8.6 %project.1 = (bf16[2,2,4,128,128]{4,3,2,1,0:T(8,128)(2,1)S(1)}, bf16[2,2,4,128,128]{4,3,2,1,0:T(8,128)(2,1)S(1)}) custom-call(bf16[256,1024]{1,0:T(8,128)(2,1)S(1)} %bitcast.10, bf16[256,1024]{1,0:T(8,128)(2,1)S(1)} %collective-permute-done.4.refs_1_, bf16[256,1024]{1,0:T(8,128)(2,1)S(1)} %collective-permute-done.5.refs_2_, ...), custom_call_target="tpu_custom_call" | custom-call | flops 4294967296 | bytes 18874368 | tf_op jit(solution)/shard_map/project/pallas_call | solution.py:120
  43.2 2.9 %collective-permute-start.10 = (bf16[1,2,2,4,128,128]{5,4,3,2,1,0:T(8,128)(2,1)S(1)}, bf16[1,2,2,4,128,128]{5,4,3,2,1,0:T(8,128)(2,1)S(1)}, u32[]{:S(2)}, u32[]{:S(2)}) collective-permute-start(bf16[1,2,2,4,128,128]{5,4,3,2,1,0:T(8,128)(2,1)S(1)} %bitcast.12), channel_id=1, source_target_pairs={{0,4},{1,5},{2,6},{3,7},{4,0},{5,1},{6,2},{7,3},{8,12},{9,13},{10,... | collective-permute-start | bytes 1572872 | tf_op jit(solution)/shard_map/ppermute | solution.py:54
  46.3 1.8 %collective-permute-done = bf16[1,256,512]{2,1,0:T(8,128)(2,1)S(1)} collective-permute-done((bf16[1,256,512]{2,1,0:T(8,128)(2,1)S(1)}, bf16[1,256,512]{2,1,0:T(8,128)(2,1)S(1)}, u32[]{:S(2)}, u32[]{:S(2)}) %collective-permute-start) | collective-permute-done | bytes 262176 | tf_op jit(solution)/shard_map/ppermute | solution.py:54
  48.1 2.9 %collective-permute-start.3 = (bf16[2,256,512]{2,1,0:T(8,128)(2,1)S(1)}, bf16[2,256,512]{2,1,0:T(8,128)(2,1)S(1)}, u32[]{:S(2)}, u32[]{:S(2)}) collective-permute-start(bf16[2,256,512]{2,1,0:T(8,128)(2,1)S(1)} %pad_maximum_fusion.1.refs_1_), channel_id=1, source_target_pairs={{0,16},{1,17},{2,18},{3,19},{4,68},{5,69},{6,70},{7,71},{8,24},{9,... | collective-permute-start | bytes 1572872 | tf_op jit(solution)/shard_map/ppermute | solution.py:54
  51.1 3.7 %collective-permute-start.13 = (bf16[2,2,2,4,128,128]{5,4,3,2,1,0:T(8,128)(2,1)S(1)}, bf16[2,2,2,4,128,128]{5,4,3,2,1,0:T(8,128)(2,1)S(1)}, u32[]{:S(2)}, u32[]{:S(2)}) collective-permute-start(bf16[2,2,2,4,128,128]{5,4,3,2,1,0:T(8,128)(2,1)S(1)} %pad_maximum_fusion.refs_5_), channel_id=1, source_target_pairs={{0,64},{1,65},{2,66},{3,67},{4,20},{5,21},{6,22},{7,23},{8,72},{9,... | collective-permute-start | bytes 3145736 | tf_op jit(solution)/shard_map/ppermute | solution.py:54
  57.1 1.5 %collective-permute-done.3.refs_4_ = bf16[2,256,512]{2,1,0:T(8,128)(2,1)S(1)} collective-permute-done((bf16[2,256,512]{2,1,0:T(8,128)(2,1)S(1)}, bf16[2,256,512]{2,1,0:T(8,128)(2,1)S(1)}, u32[]{:S(2)}, u32[]{:S(2)}) %collective-permute-start.3) | collective-permute-done | bytes 524320 | tf_op jit(solution)/shard_map/ppermute | solution.py:54
  58.6 1.3 collective-permute-start.1
  59.9 19.7 %collective-permute-done.2.refs_3_ = bf16[2,256,512]{2,1,0:T(8,128)(2,1)S(1)} collective-permute-done((bf16[2,256,512]{2,1,0:T(8,128)(2,1)S(1)}, bf16[2,256,512]{2,1,0:T(8,128)(2,1)S(1)}, u32[]{:S(2)}, u32[]{:S(2)}) %collective-permute-start.2) | collective-permute-done | bytes 524320 | tf_op jit(solution)/shard_map/ppermute | solution.py:54
  80.6 7.5 %collective-permute-done.12.refs_7_ = bf16[2,2,2,4,128,128]{5,4,3,2,1,0:T(8,128)(2,1)S(1)} collective-permute-done((bf16[2,2,2,4,128,128]{5,4,3,2,1,0:T(8,128)(2,1)S(1)}, bf16[2,2,2,4,128,128]{5,4,3,2,1,0:T(8,128)(2,1)S(1)}, u32[]{:S(2)}, u32[]{:S(2)}) %collective-permute-start.12) | collective-permute-done | bytes 1048608 | tf_op jit(solution)/shard_map/ppermute | solution.py:54
  88.1 23.8 %attend.1 = (bf16[2,544,256]{2,1,0:T(8,128)(2,1)S(1)}, bf16[2,544,256]{2,1,0:T(8,128)(2,1)S(1)}, bf16[2,544,256]{2,1,0:T(8,128)(2,1)S(1)}, bf16[2,544,256]{2,1,0:T(8,128)(2,1)S(1)}) custom-call(s32[32,32]{1,0:T(8,128)S(1)} %copy-done.3, bf16[2,256,512]{2,1,0:T(8,128)(2,1)S(1)} %pad_maximum_fusion.1.refs_1_, ...), custom_call_target="tpu_custom_call" | custom-call | tf_op jit(solution)/shard_map/attend/pallas_call | solution.py:264
  112.8 8.8 %collective-permute-start.14 = (bf16[2,544,256]{2,1,0:T(8,128)(2,1)S(1)}, bf16[2,544,256]{2,1,0:T(8,128)(2,1)S(1)}, u32[]{:S(2)}, u32[]{:S(2)}) collective-permute-start(bf16[2,544,256]{2,1,0:T(8,128)(2,1)S(1)} %get-tuple-element.14), channel_id=1, source_target_pairs={{0,24},{1,25},{2,26},{3,27},{4,100},{5,101},{6,102},{7,103},{8,0},... | collective-permute-start | bytes 1671176 | tf_op jit(solution)/shard_map/ppermute | solution.py:54
  121.6 1.2 collective-permute-start.16
  122.8 11.3 %collective-permute-done.14.b = bf16[2,544,256]{2,1,0:T(8,128)(2,1)S(1)} collective-permute-done((bf16[2,544,256]{2,1,0:T(8,128)(2,1)S(1)}, bf16[2,544,256]{2,1,0:T(8,128)(2,1)S(1)}, u32[]{:S(2)}, u32[]{:S(2)}) %collective-permute-start.14) | collective-permute-done | bytes 557088 | tf_op jit(solution)/shard_map/ppermute | solution.py:54
  134.0 3.1 %collective-permute-done.15.c = bf16[2,544,256]{2,1,0:T(8,128)(2,1)S(1)} collective-permute-done((bf16[2,544,256]{2,1,0:T(8,128)(2,1)S(1)}, bf16[2,544,256]{2,1,0:T(8,128)(2,1)S(1)}, u32[]{:S(2)}, u32[]{:S(2)}) %collective-permute-start.15) | collective-permute-done | bytes 557088 | tf_op jit(solution)/shard_map/ppermute | solution.py:54
  138.1 2.6 %merge_away.1 = bf16[256,512]{1,0:T(8,128)(2,1)} custom-call(bf16[2,544,256]{2,1,0:T(8,128)(2,1)} %copy-done.1, bf16[2,544,256]{2,1,0:T(8,128)(2,1)} %copy-done.4, bf16[2,544,256]{2,1,0:T(8,128)(2,1)} %copy-done.5, bf16[2,544,256]{2,1,0:T(8,128)(2,1)} %copy-done.6), custom_call_target="tpu_custom_call" | custom-call | tf_op jit(solution)/shard_map/merge_away/pallas_call | solution.py:319
  140.7 1.7 %collective-permute-done.17.other_ref = bf16[256,512]{1,0:T(8,128)(2,1)S(1)} collective-permute-done((bf16[256,512]{1,0:T(8,128)(2,1)}, bf16[256,512]{1,0:T(8,128)(2,1)S(1)}, u32[]{:S(2)}, u32[]{:S(2)}) %collective-permute-start.17) | collective-permute-done | bytes 262176 | tf_op jit(solution)/shard_map/ppermute | solution.py:54
  143.1 2.7 %merge_home.1 = bf16[256,1024]{1,0:T(8,128)(2,1)} custom-call(bf16[2,544,256]{2,1,0:T(8,128)(2,1)} %copy-done.1, bf16[2,544,256]{2,1,0:T(8,128)(2,1)} %copy-done.4, bf16[2,544,256]{2,1,0:T(8,128)(2,1)} %copy-done.5, bf16[2,544,256]{2,1,0:T(8,128)(2,1)} %copy-done.6, bf16[256,512]{1,0:T(8,128)(2,1)} %copy-done.8), custom_call_target="tpu_custom_call" | custom-call | tf_op jit(solution)/shard_map/merge_home/pallas_call | solution.py:327
  (38 shorter events, 9.0 us)
Async XLA Ops:
  0.0 30.1 %collective-permute-start.6 = (bf16[256,1024]{1,0:T(8,128)(2,1)}, bf16[256,1024]{1,0:T(8,128)(2,1)S(1)}, u32[]{:S(2)}, u32[]{:S(2)}) collective-permute-start(bf16[256,1024]{1,0:T(8,128)(2,1)} %bitcast.7), channel_id=1, source_target_pairs={{0,2},{1,3},{2,0},{3,1},{4,6},{5,7},{6,4},{7,5},{8,10},{9,11},{10,... | collective-permute-start | bytes 1572872 | tf_op jit(solution)/shard_map/ppermute | solution.py:54
  3.7 26.4 %collective-permute-start.5 = (bf16[256,1024]{1,0:T(8,128)(2,1)}, bf16[256,1024]{1,0:T(8,128)(2,1)S(1)}, u32[]{:S(2)}, u32[]{:S(2)}) collective-permute-start(bf16[256,1024]{1,0:T(8,128)(2,1)} %bitcast.8), channel_id=1, source_target_pairs={{0,3},{1,0},{2,1},{3,2},{4,7},{5,4},{6,5},{7,6},{8,11},{9,8},{10,9... | collective-permute-start | bytes 1572872 | tf_op jit(solution)/shard_map/ppermute | solution.py:54
  4.5 25.6 %collective-permute-start.4 = (bf16[256,1024]{1,0:T(8,128)(2,1)}, bf16[256,1024]{1,0:T(8,128)(2,1)S(1)}, u32[]{:S(2)}, u32[]{:S(2)}) collective-permute-start(bf16[256,1024]{1,0:T(8,128)(2,1)} %bitcast.9), channel_id=1, source_target_pairs={{0,1},{1,2},{2,3},{3,0},{4,5},{5,6},{6,7},{7,4},{8,9},{9,10},{10,1... | collective-permute-start | bytes 1572872 | tf_op jit(solution)/shard_map/ppermute | solution.py:54
  5.9 20.5 %collective-permute-start.9 = (bf16[1,1024]{1,0:T(2,128)(2,1)S(1)}, bf16[1,1024]{1,0:T(2,128)(2,1)S(1)}, u32[]{:S(2)}, u32[]{:S(2)}) collective-permute-start(bf16[1,1024]{1,0:T(2,128)(2,1)S(1)} %reshape.7.refs_4_), channel_id=1, source_target_pairs={{0,2},{1,3},{2,0},{3,1},{4,6},{5,7},{6,4},{7,5},{8,10},{9,11},{10,... | collective-permute-start | bytes 6152 | tf_op jit(solution)/shard_map/ppermute | solution.py:54
  6.6 21.1 %collective-permute-start.8 = (bf16[1,1024]{1,0:T(2,128)(2,1)S(1)}, bf16[1,1024]{1,0:T(2,128)(2,1)S(1)}, u32[]{:S(2)}, u32[]{:S(2)}) collective-permute-start(bf16[1,1024]{1,0:T(2,128)(2,1)S(1)} %reshape.7.refs_4_), channel_id=1, source_target_pairs={{0,3},{1,0},{2,1},{3,2},{4,7},{5,4},{6,5},{7,6},{8,11},{9,8},{10,9... | collective-permute-start | bytes 6152 | tf_op jit(solution)/shard_map/ppermute | solution.py:54
  26.4 3.7 %collective-permute-start.7 = (bf16[1,1024]{1,0:T(2,128)(2,1)S(1)}, bf16[1,1024]{1,0:T(2,128)(2,1)S(1)}, u32[]{:S(2)}, u32[]{:S(2)}) collective-permute-start(bf16[1,1024]{1,0:T(2,128)(2,1)S(1)} %reshape.7.refs_4_), channel_id=1, source_target_pairs={{0,1},{1,2},{2,3},{3,0},{4,5},{5,6},{6,7},{7,4},{8,9},{9,10},{10,1... | collective-permute-start | bytes 6152 | tf_op jit(solution)/shard_map/ppermute | solution.py:54
  30.2 3.4 %copy-start = (bf16[4096,1024]{1,0:T(8,128)(2,1)S(1)}, bf16[4096,1024]{1,0:T(8,128)(2,1)}, u32[]{:S(2)}) copy-start(bf16[4096,1024]{1,0:T(8,128)(2,1)} %refs_8_.1) | copy-start | bytes 25165828
  33.5 1.0 copy-start.2
  34.6 11.5 %copy-start.7 = (bf16[256,1024]{1,0:T(8,128)(2,1)S(1)}, bf16[256,1024]{1,0:T(8,128)(2,1)}, u32[]{:S(2)}) copy-start(bf16[256,1024]{1,0:T(8,128)(2,1)} %param.10) | copy-start | bytes 1572868
  34.6 53.5 %copy-start.3 = (s32[32,32]{1,0:T(8,128)S(1)}, s32[32,32]{1,0:T(8,128)}, u32[]{:S(2)}) copy-start(s32[32,32]{1,0:T(8,128)} %refs_0_.1) | copy-start | bytes 12292
  43.2 7.8 %collective-permute-start.10 = (bf16[1,2,2,4,128,128]{5,4,3,2,1,0:T(8,128)(2,1)S(1)}, bf16[1,2,2,4,128,128]{5,4,3,2,1,0:T(8,128)(2,1)S(1)}, u32[]{:S(2)}, u32[]{:S(2)}) collective-permute-start(bf16[1,2,2,4,128,128]{5,4,3,2,1,0:T(8,128)(2,1)S(1)} %bitcast.12), channel_id=1, source_target_pairs={{0,4},{1,5},{2,6},{3,7},{4,0},{5,1},{6,2},{7,3},{8,12},{9,13},{10,... | collective-permute-start | bytes 1572872 | tf_op jit(solution)/shard_map/ppermute | solution.py:54
  46.2 1.9 %collective-permute-start = (bf16[1,256,512]{2,1,0:T(8,128)(2,1)S(1)}, bf16[1,256,512]{2,1,0:T(8,128)(2,1)S(1)}, u32[]{:S(2)}, u32[]{:S(2)}) collective-permute-start(bf16[1,256,512]{2,1,0:T(8,128)(2,1)S(1)} %get-tuple-element.18), channel_id=1, source_target_pairs={{0,4},{1,5},{2,6},{3,7},{4,0},{5,1},{6,2},{7,3},{8,12},{9,13},{10,... | collective-permute-start | bytes 786440 | tf_op jit(solution)/shard_map/ppermute | solution.py:54
  48.1 10.5 %collective-permute-start.3 = (bf16[2,256,512]{2,1,0:T(8,128)(2,1)S(1)}, bf16[2,256,512]{2,1,0:T(8,128)(2,1)S(1)}, u32[]{:S(2)}, u32[]{:S(2)}) collective-permute-start(bf16[2,256,512]{2,1,0:T(8,128)(2,1)S(1)} %pad_maximum_fusion.1.refs_1_), channel_id=1, source_target_pairs={{0,16},{1,17},{2,18},{3,19},{4,68},{5,69},{6,70},{7,71},{8,24},{9,... | collective-permute-start | bytes 1572872 | tf_op jit(solution)/shard_map/ppermute | solution.py:54
  51.1 29.5 %collective-permute-start.13 = (bf16[2,2,2,4,128,128]{5,4,3,2,1,0:T(8,128)(2,1)S(1)}, bf16[2,2,2,4,128,128]{5,4,3,2,1,0:T(8,128)(2,1)S(1)}, u32[]{:S(2)}, u32[]{:S(2)}) collective-permute-start(bf16[2,2,2,4,128,128]{5,4,3,2,1,0:T(8,128)(2,1)S(1)} %pad_maximum_fusion.refs_5_), channel_id=1, source_target_pairs={{0,64},{1,65},{2,66},{3,67},{4,20},{5,21},{6,22},{7,23},{8,72},{9,... | collective-permute-start | bytes 3145736 | tf_op jit(solution)/shard_map/ppermute | solution.py:54
  54.7 33.3 %collective-permute-start.12 = (bf16[2,2,2,4,128,128]{5,4,3,2,1,0:T(8,128)(2,1)S(1)}, bf16[2,2,2,4,128,128]{5,4,3,2,1,0:T(8,128)(2,1)S(1)}, u32[]{:S(2)}, u32[]{:S(2)}) collective-permute-start(bf16[2,2,2,4,128,128]{5,4,3,2,1,0:T(8,128)(2,1)S(1)} %pad_maximum_fusion.refs_5_), channel_id=1, source_target_pairs={{0,96},{1,97},{2,98},{3,99},{4,28},{5,29},{6,30},{7,31},{8,104},{9... | collective-permute-start | bytes 3145736 | tf_op jit(solution)/shard_map/ppermute | solution.py:54
  55.2 32.9 %collective-permute-start.11 = (bf16[2,2,2,4,128,128]{5,4,3,2,1,0:T(8,128)(2,1)S(1)}, bf16[2,2,2,4,128,128]{5,4,3,2,1,0:T(8,128)(2,1)S(1)}, u32[]{:S(2)}, u32[]{:S(2)}) collective-permute-start(bf16[2,2,2,4,128,128]{5,4,3,2,1,0:T(8,128)(2,1)S(1)} %pad_maximum_fusion.refs_5_), channel_id=1, source_target_pairs={{0,32},{1,33},{2,34},{3,35},{4,12},{5,13},{6,14},{7,15},{8,40},{9,... | collective-permute-start | bytes 3145736 | tf_op jit(solution)/shard_map/ppermute | solution.py:54
  56.2 23.4 %collective-permute-start.2 = (bf16[2,256,512]{2,1,0:T(8,128)(2,1)S(1)}, bf16[2,256,512]{2,1,0:T(8,128)(2,1)S(1)}, u32[]{:S(2)}, u32[]{:S(2)}) collective-permute-start(bf16[2,256,512]{2,1,0:T(8,128)(2,1)S(1)} %pad_maximum_fusion.1.refs_1_), channel_id=1, source_target_pairs={{0,24},{1,25},{2,26},{3,27},{4,100},{5,101},{6,102},{7,103},{8,0},... | collective-permute-start | bytes 1572872 | tf_op jit(solution)/shard_map/ppermute | solution.py:54
  58.6 22.0 %collective-permute-start.1 = (bf16[2,256,512]{2,1,0:T(8,128)(2,1)S(1)}, bf16[2,256,512]{2,1,0:T(8,128)(2,1)S(1)}, u32[]{:S(2)}, u32[]{:S(2)}) collective-permute-start(bf16[2,256,512]{2,1,0:T(8,128)(2,1)S(1)} %pad_maximum_fusion.1.refs_1_), channel_id=1, source_target_pairs={{0,8},{1,9},{2,10},{3,11},{4,36},{5,37},{6,38},{7,39},{8,16},{9,17... | collective-permute-start | bytes 1572872 | tf_op jit(solution)/shard_map/ppermute | solution.py:54
  112.8 21.2 %collective-permute-start.14 = (bf16[2,544,256]{2,1,0:T(8,128)(2,1)S(1)}, bf16[2,544,256]{2,1,0:T(8,128)(2,1)S(1)}, u32[]{:S(2)}, u32[]{:S(2)}) collective-permute-start(bf16[2,544,256]{2,1,0:T(8,128)(2,1)S(1)} %get-tuple-element.14), channel_id=1, source_target_pairs={{0,24},{1,25},{2,26},{3,27},{4,100},{5,101},{6,102},{7,103},{8,0},... | collective-permute-start | bytes 1671176 | tf_op jit(solution)/shard_map/ppermute | solution.py:54
  121.6 15.6 %collective-permute-start.15 = (bf16[2,544,256]{2,1,0:T(8,128)(2,1)S(1)}, bf16[2,544,256]{2,1,0:T(8,128)(2,1)S(1)}, u32[]{:S(2)}, u32[]{:S(2)}) collective-permute-start(bf16[2,544,256]{2,1,0:T(8,128)(2,1)S(1)} %get-tuple-element.15), channel_id=1, source_target_pairs={{0,8},{1,9},{2,10},{3,11},{4,36},{5,37},{6,38},{7,39},{8,16},{9,17... | collective-permute-start | bytes 1671176 | tf_op jit(solution)/shard_map/ppermute | solution.py:54
  121.6 15.6 %collective-permute-start.16 = (bf16[2,544,256]{2,1,0:T(8,128)(2,1)S(1)}, bf16[2,544,256]{2,1,0:T(8,128)(2,1)S(1)}, u32[]{:S(2)}, u32[]{:S(2)}) collective-permute-start(bf16[2,544,256]{2,1,0:T(8,128)(2,1)S(1)} %get-tuple-element.16), channel_id=1, source_target_pairs={{0,16},{1,17},{2,18},{3,19},{4,68},{5,69},{6,70},{7,71},{8,24},{9,... | collective-permute-start | bytes 1671176 | tf_op jit(solution)/shard_map/ppermute | solution.py:54
  134.0 3.1 %copy-start.4 = (bf16[2,544,256]{2,1,0:T(8,128)(2,1)}, bf16[2,544,256]{2,1,0:T(8,128)(2,1)S(1)}, u32[]{:S(2)}) copy-start(bf16[2,544,256]{2,1,0:T(8,128)(2,1)S(1)} %collective-permute-done.14.b) | copy-start | bytes 1671172
  137.1 1.0 copy-start.6
  140.7 1.7 %collective-permute-start.17 = (bf16[256,512]{1,0:T(8,128)(2,1)}, bf16[256,512]{1,0:T(8,128)(2,1)S(1)}, u32[]{:S(2)}, u32[]{:S(2)}) collective-permute-start(bf16[256,512]{1,0:T(8,128)(2,1)} %merge_away.1), channel_id=1, source_target_pairs={{0,4},{1,5},{2,6},{3,7},{4,0},{5,1},{6,2},{7,3},{8,12},{9,13},{10,... | collective-permute-start | bytes 786440 | tf_op jit(solution)/shard_map/ppermute | solution.py:54
  (3 other events, 2.3 us)

commit v2 on v0

v2 whole, which is shorter than its diff:
```python
import functools

import jax
import jax.numpy as jnp
from jax import lax
from jax.experimental import pallas as pl
from jax.experimental.pallas import tpu as pltpu
from jax.sharding import PartitionSpec as P

AXES = ("dp", "mp")
SIDE = 4
HD = 64
BLOCK = 128
ROWS = 2 * BLOCK
HALF = 512
PAIRS = 4
PART = 2
TILE = 128
QTOK = 256
STAT = 32
SUMS = TILE + 16
LOW = -1e30
OFFSETS = (0, 3, 1, 2)
F32, BF16 = jnp.float32, jnp.bfloat16
MIB = 2**20


def device_id(x, y, z, c):
    return ((x * SIDE + z) * 2 + c) * SIDE + y


def permutation(move):
    pairs = []
    for x in range(SIDE):
        for z in range(SIDE):
            for c in range(2):
                for y in range(SIDE):
                    pairs.append((device_id(x, y, z, c), device_id(*move(x, y, z, c))))
    return pairs


def along_y(step):
    return permutation(lambda x, y, z, c: (x, (y + step) % SIDE, z, c))


def along_ring(step, first_along_x, cross=0):
    def move(x, y, z, c):
        if (c == 0) == first_along_x:
            return ((x + step) % SIDE, y, z, c ^ cross)
        return (x, y, (z + step) % SIDE, c ^ cross)

    return permutation(move)


CORE_SWAP = permutation(lambda x, y, z, c: (x, y, z, 1 - c))


def send(array, pairs):
    return lax.ppermute(array, AXES, pairs)


def gather(array, ring):
    far = send(array, ring(2))
    return [array, send(array, ring(1)), send(array, ring(-1)), far]


def place():
    index = lax.axis_index("dp")
    return index >> 3, (index >> 1) & 3, index & 1


def vmem():
    return pl.BlockSpec(memory_space=pltpu.VMEM)


def anywhere():
    return pl.BlockSpec(memory_space=pl.ANY)


def preload_kernel(key_hbm, value_hbm, key_out, value_out, sems):
    copies = [
        pltpu.make_async_copy(key_hbm, key_out, sems.at[0]),
        pltpu.make_async_copy(value_hbm, value_out, sems.at[1]),
    ]
    for copy in copies:
        copy.start()
    for copy in copies:
        copy.wait()


def preload(key_weight, value_weight):
    return pl.pallas_call(
        preload_kernel,
        out_shape=(pltpu.VMEM(key_weight.shape, BF16),) * 2,
        in_specs=[anywhere()] * 2,
        out_specs=(vmem(),) * 2,
        scratch_shapes=[pltpu.SemaphoreType.DMA((2,))],
        compiler_params=pltpu.CompilerParams(vmem_limit_bytes=20 * MIB),
        cost_estimate=pl.CostEstimate(flops=0, bytes_accessed=1024, transcendentals=0),
        name="preload",
    )(key_weight, value_weight)


def normalise(x_refs, gain_refs, normed):
    width = x_refs[0].shape[1]
    for block in range(2):
        rows = pl.ds(block * BLOCK, BLOCK)
        parts = [x_ref[rows, :] for x_ref in x_refs[:3]] + [x_refs[3 + block][...]]
        total = jnp.zeros((BLOCK, 1), F32)
        for part in parts:
            floats = part.astype(F32)
            total += jnp.sum(floats * floats, axis=-1, keepdims=True)
        scale = lax.rsqrt(total * (1.0 / (4 * width)) + 1e-06)
        for slot, part in enumerate(parts):
            gain = gain_refs[slot][...].reshape(1, width).astype(F32)
            normed[slot, rows, :] = (part.astype(F32) * scale * gain).astype(BF16)


def project_kernel(part, *refs):
    refs = list(refs)
    if part == 0:
        x_refs = [refs.pop(0) for _ in range(5)]
        gain_refs = [refs.pop(0) for _ in range(4)]
    else:
        normed = refs.pop(0)
    weight_refs = [refs.pop(0) for _ in range(2)]
    mine_ref, away_ref = refs[0:2]
    if part == 0:
        normed = refs[2]
        normalise(x_refs, gain_refs, normed)
    width = normed.shape[2]
    columns = PART * TILE
    y = lax.axis_index("mp")
    core = place()[2]
    for half, out_ref in enumerate((away_ref, mine_ref)):
        column = pl.multiple_of((core ^ (1 - half)) * HALF + part * columns, columns)
        for which in range(2):
            product = jnp.zeros((ROWS, columns), F32)
            for slot in range(4):
                row = pl.multiple_of(((y + OFFSETS[slot]) & 3) * width, width)
                product += jnp.dot(
                    normed[slot],
                    weight_refs[which][pl.ds(row, width), pl.ds(column, columns)],
                    preferred_element_type=F32,
                )
            for block in range(2):
                for pair in range(PART):
                    tile = product[
                        block * BLOCK : (block + 1) * BLOCK, pair * TILE : (pair + 1) * TILE
                    ]
                    if which == 1:
                        tile = tile.T
                    out_ref[block, which, pair] = tile.astype(BF16)


def project(part, inputs, key_weight, value_weight):
    shapes = [jax.ShapeDtypeStruct((2, 2, PART, TILE, BLOCK), BF16)] * 2
    if part == 0:
        shapes.append(jax.ShapeDtypeStruct((4, ROWS, inputs[0].shape[1]), BF16))
    return pl.pallas_call(
        functools.partial(project_kernel, part),
        out_shape=tuple(shapes),
        in_specs=[vmem()] * (len(inputs) + 2),
        out_specs=(vmem(),) * len(shapes),
        compiler_params=pltpu.CompilerParams(vmem_limit_bytes=28 * MIB),
        cost_estimate=pl.CostEstimate(flops=0, bytes_accessed=1024, transcendentals=0),
        name="project",
    )(*inputs, key_weight, value_weight)


def spread(top):
    def rows(pair):
        a = top[2 * pair : 2 * pair + 1]
        b = top[2 * pair + 1 : 2 * pair + 2]
        return jnp.concatenate(
            [
                jnp.broadcast_to(a, (HD, QTOK)),
                jnp.broadcast_to(b, (HD, QTOK)),
                jnp.broadcast_to(a, (8, QTOK)),
                jnp.broadcast_to(b, (8, QTOK)),
            ],
            axis=0,
        )

    return rows


def attend_kernel(part, slots, *refs):
    refs = list(refs)
    take = lambda n: [refs.pop(0) for _ in range(n)]
    wanted = refs.pop(0)
    q_hbm, kv_hbm = take(len(slots)), take(4)
    if part:
        early_out, early_stats = take(2)
        outs = take(2 * len(slots))
    else:
        early_out, early_stats = take(2)
    qbuf, kvbuf, masked, scores, run_sums, run_tops, chosen, in_sems = take(8)
    x, z, core = place()
    columns = pl.ds(part * PART * TILE, PART * TILE)
    copies = []
    for number in range(len(slots)):
        copies.append(
            pltpu.make_async_copy(
                q_hbm[number].at[:, :, columns],
                qbuf.at[pl.ds(2 * number, 2)],
                in_sems.at[4 + number],
            )
        )
    for t in range(4):
        copies.append(
            pltpu.make_async_copy(kv_hbm[t], kvbuf.at[pl.ds(2 * t, 2)], in_sems.at[t])
        )
    for copy in copies:
        copy.start()
    for copy in copies:
        copy.wait()

    def dp_index(along_x, offset, swapped):
        ex = jnp.where(along_x, (x + offset) & 3, x)
        ez = jnp.where(along_x, z, (z + offset) & 3)
        return (ex * 4 + ez) * 2 + (core ^ swapped)

    lane_half = lax.broadcasted_iota(jnp.int32, (QTOK, TILE), 1) // HD
    row = lax.broadcasted_iota(jnp.int32, (16, 2 * BLOCK), 0) // 8
    col = lax.broadcasted_iota(jnp.int32, (16, 2 * BLOCK), 1) // BLOCK
    ones = jnp.where(row == col, 1.0, 0.0).astype(BF16)
    empty = jnp.zeros((HD, BLOCK), BF16)

    def question(index, carry):
        number = index >> 1
        offset, offset_slot = jnp.int32(OFFSETS[slots[0]]), jnp.int32(slots[0])
        for other in range(1, len(slots)):
            offset = jnp.where(number == other, OFFSETS[slots[other]], offset)
            offset_slot = jnp.where(number == other, slots[other], offset_slot)
        q_index = dp_index(core == 1, offset, index & 1)
        count = jnp.int32(0)
        for t in range(4):
            for swapped in range(2):
                local = wanted[q_index, dp_index(core == 0, OFFSETS[t], swapped)]
                chosen[count] = (t * 2 + swapped) * 2 + jnp.maximum(local, 0)
                count = count + jnp.where(local >= 0, 1, 0)
        for pair in range(PART):
            query = qbuf[index, :, pair * TILE : (pair + 1) * TILE]
            for head in range(2):
                masked[pair, head] = jnp.where(lane_half == head, query, jnp.zeros_like(query))
        run_sums[...] = jnp.zeros((PART, SUMS, QTOK), F32)
        run_tops[...] = jnp.full((8, QTOK), LOW, F32)
        chosen[count] = chosen[jnp.maximum(count - 1, 0)]

        def weigh(size):
            places = [chosen[step] for step in range(size)]
            live = (count == size).astype(BF16)
            rows = []
            for pair in range(PART):
                keys = [kvbuf[where >> 1, where & 1, 0, pair] for where in places]
                keys = jnp.concatenate(keys, axis=0)
                for head in range(2):
                    s = lax.dot_general(
                        keys,
                        masked[pair, head],
                        (((1,), (1,)), ((), ())),
                        preferred_element_type=F32,
                    )
                    rows.append(jnp.max(s, axis=0, keepdims=True))
                    scores[:size, pair, head] = s.reshape(size, BLOCK, QTOK)
            run_tops[...] = jnp.concatenate(rows + rows, axis=0)
            for pair in range(PART):
                left, probs = [], []
                for step, where in enumerate(places):
                    for head in range(2):
                        shifted = scores[step, pair, head] - rows[2 * pair + head]
                        probs.append(jnp.exp(shifted).astype(BF16))
                    values, unit = kvbuf[where >> 1, where & 1, 1, pair], ones
                    if step == size - 1:
                        values, unit = values * live, unit * live
                    left.append(
                        jnp.concatenate(
                            [
                                jnp.concatenate([values[:HD], empty], axis=1),
                                jnp.concatenate([empty, values[HD:]], axis=1),
                                unit,
                            ],
                            axis=0,
                        )
                    )
                run_sums[pair] = jnp.dot(
                    jnp.concatenate(left, axis=1),
                    jnp.concatenate(probs, axis=0),
                    preferred_element_type=F32,
                )

        for size in (2, 4, 6, 8):

            @pl.when((count + 1) >> 1 == size // 2)
            def _(size=size):
                weigh(size)

        tops = run_tops[...]
        totals = []
        finished = []
        for pair in range(PART):
            done = run_sums[pair]
            finished.append(done)
            totals += [done[TILE : TILE + 1], done[TILE + 8 : TILE + 9]]
        total = jnp.concatenate(totals, axis=0)
        some = total > 0.0
        safe = jnp.where(some, total, 1.0)
        inverse = spread(1.0 / safe)
        pieces = [(done * inverse(pair))[:TILE].astype(BF16) for pair, done in enumerate(finished)]
        stat = jnp.where(some, tops[: 2 * PART] + jnp.log(safe), LOW)
        if part == 0:
            early_out[index] = jnp.concatenate(pieces, axis=0)
            early_stats[index] = jnp.concatenate([stat, stat], axis=0)
            return carry
        early = 2 * offset_slot + (index & 1)
        rest = jnp.concatenate([early_stats[early][: 2 * PART], stat], axis=0)
        pieces = [early_out[early]] + pieces
        stats = []
        for _ in range(3):
            rounded = rest.astype(BF16).astype(F32)
            stats.append(rounded)
            rest = rest - rounded
        stats.append(jnp.zeros_like(rest))
        pieces.append(jnp.concatenate(stats, axis=0).astype(BF16))
        message = jnp.concatenate(pieces, axis=0)
        for other in range(2 * len(slots)):

            @pl.when(index == other)
            def _(other=other):
                outs[other][...] = message

        return carry

    lax.fori_loop(0, 2 * len(slots), question, 0)


def attend(part, wanted, queries, blocks, slots, early=()):
    count = 2 * len(slots)
    if part:
        out_shape = (jax.ShapeDtypeStruct((HALF + STAT, QTOK), BF16),) * count
    else:
        out_shape = (
            jax.ShapeDtypeStruct((count, PART * TILE, QTOK), BF16),
            jax.ShapeDtypeStruct((count, 8, QTOK), F32),
        )
    return pl.pallas_call(
        functools.partial(attend_kernel, part, slots),
        out_shape=out_shape,
        in_specs=[pl.BlockSpec(memory_space=pltpu.SMEM)]
        + [anywhere()] * (len(slots) + 4)
        + [vmem()] * len(early),
        out_specs=(vmem(),) * len(out_shape),
        scratch_shapes=[
            pltpu.VMEM((count, QTOK, PART * TILE), BF16),
            pltpu.VMEM((8, 2, 2, PART, TILE, BLOCK), BF16),
            pltpu.VMEM((PART, 2, QTOK, TILE), BF16),
            pltpu.VMEM((8, PART, 2, BLOCK, QTOK), F32),
            pltpu.VMEM((PART, SUMS, QTOK), F32),
            pltpu.VMEM((8, QTOK), F32),
            pltpu.SMEM((16,), jnp.int32),
            pltpu.SemaphoreType.DMA((4 + len(slots),)),
        ],
        compiler_params=pltpu.CompilerParams(vmem_limit_bytes=24 * MIB),
        cost_estimate=pl.CostEstimate(
            flops=count * 10**9, bytes_accessed=8 * MIB, transcendentals=0
        ),
        name="attend",
    )(wanted, *[queries[slot] for slot in slots], *blocks, *early)


def merged(refs):
    stats = []
    for ref in refs:
        stat = ref[HALF : HALF + STAT, :].astype(F32)
        stats.append(stat[0:8] + stat[8:16] + stat[16:24])
    top = functools.reduce(jnp.maximum, stats)
    weights = [jnp.exp(stat - top) for stat in stats]
    inverse = 1.0 / sum(weights)
    weights = [weight * inverse for weight in weights]
    heads = []
    for head in range(2 * PAIRS):
        heads.append(
            sum(
                ref[head * HD : (head + 1) * HD, :].astype(F32) * weight[head : head + 1]
                for ref, weight in zip(refs, weights)
            ).astype(BF16)
        )
    row = lax.broadcasted_iota(jnp.int32, (QTOK, QTOK), 0)
    col = lax.broadcasted_iota(jnp.int32, (QTOK, QTOK), 1)
    unit = jnp.where(row == col, 1.0, 0.0).astype(BF16)
    return lax.dot_general(
        unit,
        jnp.concatenate(heads, axis=0),
        (((1,), (1,)), ((), ())),
        preferred_element_type=F32,
    )


def merge_kernel(*refs):
    out_ref = refs[8]
    core = place()[2]
    for half in range(2):
        column = pl.multiple_of((core ^ half) * HALF, HALF)
        out_ref[:, pl.ds(column, HALF)] = merged(refs[4 * half : 4 * half + 4]).astype(BF16)


def merge(mine, away):
    return pl.pallas_call(
        merge_kernel,
        out_shape=jax.ShapeDtypeStruct((QTOK, 2 * HALF), BF16),
        in_specs=[vmem()] * 8,
        out_specs=vmem(),
        compiler_params=pltpu.CompilerParams(vmem_limit_bytes=16 * MIB),
        name="merge",
    )(*mine, *away)


def both_cores(mine, away):
    return jnp.concatenate([mine[None], send(away, CORE_SWAP)[None]], axis=0)


def local(block_states, norm_gain, key_weight, value_weight, queries, wanted):
    kv_ring = functools.partial(along_ring, first_along_x=True)
    q_ring = functools.partial(along_ring, first_along_x=False)
    core = place()[2]
    own = block_states.reshape(ROWS, block_states.shape[2])
    left, right = send(own, along_y(1)), send(own, along_y(-1))
    gains = gather(norm_gain, along_y)
    mine = lax.dynamic_slice_in_dim(queries, core * HALF, HALF, 1)
    away = lax.dynamic_slice_in_dim(queries, (1 - core) * HALF, HALF, 1)
    slots_q = gather(both_cores(mine, away), q_ring)
    key_weight, value_weight = preload(key_weight, value_weight)
    far = [send(left[:BLOCK], along_y(1)), send(right[BLOCK:], along_y(-1))]
    *slots_q, far[1] = lax.optimization_barrier((*slots_q, far[1]))
    inputs = [own, left, right, *far, *gains]
    *ready, normed = project(0, inputs, key_weight, value_weight)
    kv = gather(both_cores(*ready), kv_ring)
    kv_late = gather(both_cores(*project(1, [normed], key_weight, value_weight)), kv_ring)
    early = attend(0, wanted, slots_q, kv, (0, 1, 2, 3))
    mine, away = [], []
    for slots in ((3, 1), (2,), (0,)):
        outs = attend(1, wanted, slots_q, kv_late, slots, early)
        for number, slot in enumerate(slots):
            same, cross = outs[2 * number : 2 * number + 2]
            step = OFFSETS[slot]
            mine.append(send(same, q_ring(step)) if slot else same)
            away.append(send(cross, q_ring(step, cross=1)))
    return merge(mine, away)


def solution(mesh):
    return jax.shard_map(
        local,
        mesh=mesh,
        in_specs=(P("dp", None, "mp"), P("mp"), P(None, "mp"), P(None, "mp"), P("dp", "mp"), P()),
        out_specs=P("dp", "mp"),
        check_vma=False,
    )
```

time: 471 us -> 96.7 us (0.21)
  local copies, waits for them, and re-layouts: 163 us -> 7.87 us
  waiting for transfers between devices: 140 us -> 20.4 us
  matrix products: 97.2 us -> 0 us
  other arithmetic: 44.3 us -> 0.15 us
  starting transfers between devices: 0.04 us -> 39.2 us
  Pallas kernels: 0 us -> 28.5 us
  between operations: 13.6 us -> 0.19 us
  blocking collectives: 9.56 us -> 0 us
    all_gather x2 -> x0, waiting for transfers between devices: 139 us -> none  [the longest x1 113 us: local(): piece_kv = lax.all_gather(kv_pairs, 'dp', axis=0, tiled=True)]
    dynamic_slice x32 -> x0, local copies, waits for them, and re-layouts: 100 us -> none  [sweep_blocks(): running, _ = lax.scan(scan_step, running, (shaped, usable_groups))]
    dot_general x34 -> x0, matrix products: 97.2 us -> none  [the longest x16 46.9 us: attend(): jnp.einsum('hqk,khd->hqd', weights, value_part, preferred_element_type=jn...]
    ppermute x0 -> x26, starting transfers between devices: none -> 39.2 us  [send(): return lax.ppermute(array, AXES, pairs)]
    reduce_sum x17 -> x0, other arithmetic: 39 us -> none  [the longest x16 36.9 us: attend(): jnp.sum(weights.astype(jnp.float32), axis=-1)]
    reshape x32 -> x0, local copies, waits for them, and re-layouts: 30.5 us -> none  [the longest x16 23.4 us: attend(): key_part = blocks[:, :, :cols].reshape(key_count, head_count, HD)]
    pallas_call x0 -> x8, Pallas kernels: none -> 28.5 us  [the longest x4 20 us: attend(): pl.pallas_call(functools.partial(attend_kernel, part, slots), out_shape=o...]
    slice x16 -> x2, local copies, waits for them, and re-layouts: 27.3 us -> 0.04 us  [local(): far = [send(left[:BLOCK], along_y(1)), send(right[BLOCK:], along_y(-1))]]
  transfers between devices with their start and end apart: 2 -> 26, of which waited for: 2 -> 7; matrix products, arithmetic and copies ran while one was open for 0% -> 0% of each run, Pallas kernels for 0% -> 21%
where the time goes in v2:
time: 96.7 us; the launch traced here: 96.2 us
  starting transfers between devices  39.2 us (41%)
  Pallas kernels  28.5 us (29%)
  waiting for transfers between devices  20.4 us (21%)
  local copies, waits for them, and re-layouts  7.87 us (8%)
    ppermute x26, starting transfers between devices, send(): return lax.ppermute(array, AXES, pairs)  39.2 us
    ppermute x26, waiting for transfers between devices, send(): return lax.ppermute(array, AXES, pairs)  20.4 us
    pallas_call x4, Pallas kernels, attend(): pl.pallas_call(functools.partial(attend_kernel, part, slots), out_shape=o...  20 us
    unnamed x10, local copies, waits for them, and re-layouts  6.77 us
    pallas_call x2, Pallas kernels, project(): pl.pallas_call(functools.partial(project_kernel, part), out_shape=tuple(s...  5.86 us
  transfers between devices with their start and end apart: 26, of which 7 were waited for; matrix products, arithmetic and copies ran while one was open for 0% of the time, Pallas kernels for 21%

profile of v2, /device:TPU:1, one launch (start us, length us, event | category | flops | bytes accessed | tf_op | source)
XLA Modules:
  0.0 96.2 jit_solution(10861801089548010881)
XLA Ops:
  2.6 2.8 %collective-permute-start.4 = (bf16[256,1024]{1,0:T(8,128)(2,1)}, bf16[256,1024]{1,0:T(8,128)(2,1)S(1)}, u32[]{:S(2)}, u32[]{:S(2)}) collective-permute-start(bf16[256,1024]{1,0:T(8,128)(2,1)} %bitcast.8), channel_id=1, source_target_pairs={{0,3},{1,0},{2,1},{3,2},{4,7},{5,4},{6,5},{7,6},{8,11},{9,8},{10,9... | collective-permute-start | bytes 1572872 | tf_op jit(solution)/shard_map/ppermute | solution.py:59
  5.5 2.8 %collective-permute-start.3 = (bf16[2,256,512]{2,1,0:T(8,128)(2,1)S(1)}, bf16[2,256,512]{2,1,0:T(8,128)(2,1)S(1)}, u32[]{:S(2)}, u32[]{:S(2)}) collective-permute-start(bf16[2,256,512]{2,1,0:T(8,128)(2,1)S(1)} %pad_maximum_fusion.refs_1_), channel_id=1, source_target_pairs={{0,16},{1,17},{2,18},{3,19},{4,68},{5,69},{6,70},{7,71},{8,24},{9,... | collective-permute-start | bytes 1572872 | tf_op jit(solution)/shard_map/ppermute | solution.py:59
  9.8 7.2 %collective-permute-done.4.refs_2_ = bf16[256,1024]{1,0:T(8,128)(2,1)S(1)} collective-permute-done((bf16[256,1024]{1,0:T(8,128)(2,1)}, bf16[256,1024]{1,0:T(8,128)(2,1)S(1)}, u32[]{:S(2)}, u32[]{:S(2)}) %collective-permute-start.4) | collective-permute-done | bytes 524320 | tf_op jit(solution)/shard_map/ppermute | solution.py:59
  17.0 3.4 %collective-permute-start.5 = (bf16[128,1024]{1,0:T(8,128)(2,1)S(1)}, bf16[128,1024]{1,0:T(8,128)(2,1)S(1)}, u32[]{:S(2)}, u32[]{:S(2)}) collective-permute-start(bf16[128,1024]{1,0:T(8,128)(2,1)S(1)} %slice.8), channel_id=1, source_target_pairs={{0,3},{1,0},{2,1},{3,2},{4,7},{5,4},{6,5},{7,6},{8,11},{9,8},{10,9... | collective-permute-start | bytes 786440 | tf_op jit(solution)/shard_map/ppermute | solution.py:59
  20.5 2.7 %collective-permute-start.9 = (bf16[1024]{0:T(1024)(128)(2,1)}, bf16[1024]{0:T(1024)(128)(2,1)S(1)}, u32[]{:S(2)}, u32[]{:S(2)}) collective-permute-start(bf16[1024]{0:T(1024)(128)(2,1)} %refs_5_.1), channel_id=1, source_target_pairs={{0,3},{1,0},{2,1},{3,2},{4,7},{5,4},{6,5},{7,6},{8,11},{9,8},{10,9... | collective-permute-start | bytes 6152 | tf_op jit(solution)/shard_map/ppermute | solution.py:59
  23.2 1.8 %collective-permute-start.10 = (bf16[1024]{0:T(1024)(128)(2,1)}, bf16[1024]{0:T(1024)(128)(2,1)S(1)}, u32[]{:S(2)}, u32[]{:S(2)}) collective-permute-start(bf16[1024]{0:T(1024)(128)(2,1)} %refs_5_.1), channel_id=1, source_target_pairs={{0,2},{1,3},{2,0},{3,1},{4,6},{5,7},{6,4},{7,5},{8,10},{9,11},{10,... | collective-permute-start | bytes 6152 | tf_op jit(solution)/shard_map/ppermute | solution.py:59
  25.0 3.4 %copy-done = bf16[4096,1024]{1,0:T(8,128)(2,1)S(1)} copy-done((bf16[4096,1024]{1,0:T(8,128)(2,1)S(1)}, bf16[4096,1024]{1,0:T(8,128)(2,1)}, u32[]{:S(2)}) %copy-start) | copy-done | bytes 8388632
  28.4 3.4 %copy-done.1 = bf16[4096,1024]{1,0:T(8,128)(2,1)S(1)} copy-done((bf16[4096,1024]{1,0:T(8,128)(2,1)S(1)}, bf16[4096,1024]{1,0:T(8,128)(2,1)}, u32[]{:S(2)}) %copy-start.1) | copy-done | bytes 8388632
  33.0 3.3 %project.2 = (bf16[2,2,2,128,128]{4,3,2,1,0:T(8,128)(2,1)S(1)}, bf16[2,2,2,128,128]{4,3,2,1,0:T(8,128)(2,1)S(1)}, bf16[4,256,1024]{2,1,0:T(8,128)(2,1)S(1)}) custom-call(bf16[256,1024]{1,0:T(8,128)(2,1)S(1)} %bitcast.10, bf16[256,1024]{1,0:T(8,128)(2,1)S(1)} %collective-permute-done.6.refs_1_, bf16[256,1024]{1,0:T(8,128)(2,1)S(1)} %collective-permute-done.4.refs_2_, ...), custom_call_target="tpu_custom_call" | custom-call | bytes 1024 | tf_op jit(solution)/shard_map/project/pallas_call | solution.py:160
  36.3 3.4 %collective-permute-start.15 = (bf16[2,2,2,128,128]{4,3,2,1,0:T(8,128)(2,1)S(1)}, bf16[2,2,2,128,128]{4,3,2,1,0:T(8,128)(2,1)S(1)}, u32[]{:S(2)}, u32[]{:S(2)}) collective-permute-start(bf16[2,2,2,128,128]{4,3,2,1,0:T(8,128)(2,1)S(1)} %get-tuple-element.38), channel_id=1, source_target_pairs={{0,4},{1,5},{2,6},{3,7},{4,0},{5,1},{6,2},{7,3},{8,12},{9,13},{10,... | collective-permute-start | bytes 786440 | tf_op jit(solution)/shard_map/ppermute | solution.py:59
  40.9 1.8 %collective-permute-start.18 = (bf16[2,2,2,2,128,128]{5,4,3,2,1,0:T(8,128)(2,1)S(1)}, bf16[2,2,2,2,128,128]{5,4,3,2,1,0:T(8,128)(2,1)S(1)}, u32[]{:S(2)}, u32[]{:S(2)}) collective-permute-start(bf16[2,2,2,2,128,128]{5,4,3,2,1,0:T(8,128)(2,1)S(1)} %pad_maximum_fusion.2.refs_5_), channel_id=1, source_target_pairs={{0,64},{1,65},{2,66},{3,67},{4,20},{5,21},{6,22},{7,23},{8,72},{9,... | collective-permute-start | bytes 1572872 | tf_op jit(solution)/shard_map/ppermute | solution.py:59
  44.2 2.5 %project.3 = (bf16[2,2,2,128,128]{4,3,2,1,0:T(8,128)(2,1)S(1)}, bf16[2,2,2,128,128]{4,3,2,1,0:T(8,128)(2,1)S(1)}) custom-call(bf16[4,256,1024]{2,1,0:T(8,128)(2,1)S(1)} %get-tuple-element.32.refs_0_, bf16[4096,1024]{1,0:T(8,128)(2,1)S(1)} %get-tuple-element.30.refs_9_.refs_1_, bf16[4096,1024]{1,0:T(8,128)(2,1)S(1)} %get-tuple-element.31.refs_10_.refs_2_), custom_call_target="tpu_custom_call" | custom-call | bytes 1024 | tf_op jit(solution)/shard_map/project/pallas_call | solution.py:160
  46.7 2.3 %collective-permute-start.11 = (bf16[2,2,2,128,128]{4,3,2,1,0:T(8,128)(2,1)S(1)}, bf16[2,2,2,128,128]{4,3,2,1,0:T(8,128)(2,1)S(1)}, u32[]{:S(2)}, u32[]{:S(2)}) collective-permute-start(bf16[2,2,2,128,128]{4,3,2,1,0:T(8,128)(2,1)S(1)} %get-tuple-element.34), channel_id=1, source_target_pairs={{0,4},{1,5},{2,6},{3,7},{4,0},{5,1},{6,2},{7,3},{8,12},{9,13},{10,... | collective-permute-start | bytes 786440 | tf_op jit(solution)/shard_map/ppermute | solution.py:59
  50.2 1.8 %collective-permute-start.14 = (bf16[2,2,2,2,128,128]{5,4,3,2,1,0:T(8,128)(2,1)S(1)}, bf16[2,2,2,2,128,128]{5,4,3,2,1,0:T(8,128)(2,1)S(1)}, u32[]{:S(2)}, u32[]{:S(2)}) collective-permute-start(bf16[2,2,2,2,128,128]{5,4,3,2,1,0:T(8,128)(2,1)S(1)} %pad_maximum_fusion.1.refs_3_.refs_2_), channel_id=1, source_target_pairs={{0,64},{1,65},{2,66},{3,67},{4,20},{5,21},{6,22},{7,23},{8,72},{9,... | collective-permute-start | bytes 1572872 | tf_op jit(solution)/shard_map/ppermute | solution.py:59
  53.5 3.0 %collective-permute-done.17.refs_7_ = bf16[2,2,2,2,128,128]{5,4,3,2,1,0:T(8,128)(2,1)S(1)} collective-permute-done((bf16[2,2,2,2,128,128]{5,4,3,2,1,0:T(8,128)(2,1)S(1)}, bf16[2,2,2,2,128,128]{5,4,3,2,1,0:T(8,128)(2,1)S(1)}, u32[]{:S(2)}, u32[]{:S(2)}) %collective-permute-start.17) | collective-permute-done | bytes 524320 | tf_op jit(solution)/shard_map/ppermute | solution.py:59
  56.5 8.9 %attend.4 = (bf16[8,256,256]{2,1,0:T(8,128)(2,1)S(1)}, f32[8,8,256]{2,1,0:T(8,128)S(1)}) custom-call(s32[32,32]{1,0:T(8,128)S(1)} %copy-done.4, bf16[2,256,512]{2,1,0:T(8,128)(2,1)S(1)} %pad_maximum_fusion.refs_1_, bf16[2,256,512]{2,1,0:T(8,128)(2,1)S(1)} %collective-permute-done.1.refs_2_, bf16[2,256,512]{2,1,0:T(8,128)(2,1)S(1)} %collective-permute-done.2.refs_3_.refs_1_, ...), custom_call_target="tpu_custom_call" | custom-call | flops 8000000000 | bytes 8388608 | tf_op jit(solution)/shard_map/attend/pallas_call | solution.py:347
  65.4 2.4 %collective-permute-done.13.refs_5_.refs_4_ = bf16[2,2,2,2,128,128]{5,4,3,2,1,0:T(8,128)(2,1)S(1)} collective-permute-done((bf16[2,2,2,2,128,128]{5,4,3,2,1,0:T(8,128)(2,1)S(1)}, bf16[2,2,2,2,128,128]{5,4,3,2,1,0:T(8,128)(2,1)S(1)}, u32[]{:S(2)}, u32[]{:S(2)}) %collective-permute-start.13) | collective-permute-done | bytes 524320 | tf_op jit(solution)/shard_map/ppermute | solution.py:59
  67.7 3.1 %attend.6 = (bf16[544,256]{1,0:T(8,128)(2,1)S(1)}, bf16[544,256]{1,0:T(8,128)(2,1)S(1)}) custom-call(s32[32,32]{1,0:T(8,128)S(1)} %copy-done.4, bf16[2,256,512]{2,1,0:T(8,128)(2,1)S(1)} %collective-permute-done.2.refs_3_.refs_1_, bf16[2,2,2,2,128,128]{5,4,3,2,1,0:T(8,128)(2,1)S(1)} %pad_maximum_fusion.1.refs_3_.refs_2_, ...), custom_call_target="tpu_custom_call" | custom-call | flops 2000000000 | bytes 8388608 | tf_op jit(solution)/shard_map/attend/pallas_call | solution.py:347
  70.9 1.5 %collective-permute-start.21 = (bf16[544,256]{1,0:T(8,128)(2,1)S(1)}, bf16[544,256]{1,0:T(8,128)(2,1)S(1)}, u32[]{:S(2)}, u32[]{:S(2)}) collective-permute-start(bf16[544,256]{1,0:T(8,128)(2,1)S(1)} %get-tuple-element.43), channel_id=1, source_target_pairs={{0,8},{1,9},{2,10},{3,11},{4,36},{5,37},{6,38},{7,39},{8,16},{9,17... | collective-permute-start | bytes 835592 | tf_op jit(solution)/shard_map/ppermute | solution.py:59
  73.8 4.9 %attend.5 = (bf16[544,256]{1,0:T(8,128)(2,1)S(1)}, bf16[544,256]{1,0:T(8,128)(2,1)S(1)}, bf16[544,256]{1,0:T(8,128)(2,1)S(1)}, bf16[544,256]{1,0:T(8,128)(2,1)S(1)}) custom-call(s32[32,32]{1,0:T(8,128)S(1)} %copy-done.4, bf16[2,256,512]{2,1,0:T(8,128)(2,1)S(1)} %collective-permute-done.3.refs_4_.refs_1_, ...), custom_call_target="tpu_custom_call" | custom-call | flops 4000000000 | bytes 8388608 | tf_op jit(solution)/shard_map/attend/pallas_call | solution.py:347
  78.7 2.9 %collective-permute-start.19 = (bf16[544,256]{1,0:T(8,128)(2,1)S(1)}, bf16[544,256]{1,0:T(8,128)(2,1)S(1)}, u32[]{:S(2)}, u32[]{:S(2)}) collective-permute-start(bf16[544,256]{1,0:T(8,128)(2,1)S(1)} %get-tuple-element.41), channel_id=1, source_target_pairs={{0,16},{1,17},{2,18},{3,19},{4,68},{5,69},{6,70},{7,71},{8,24},{9,... | collective-permute-start | bytes 835592 | tf_op jit(solution)/shard_map/ppermute | solution.py:59
  82.9 2.1 %collective-permute-start.22 = (bf16[544,256]{1,0:T(8,128)(2,1)S(1)}, bf16[544,256]{1,0:T(8,128)(2,1)S(1)}, u32[]{:S(2)}, u32[]{:S(2)}) collective-permute-start(bf16[544,256]{1,0:T(8,128)(2,1)S(1)} %get-tuple-element.45), channel_id=1, source_target_pairs={{0,20},{1,21},{2,22},{3,23},{4,64},{5,65},{6,66},{7,67},{8,28},{9,... | collective-permute-start | bytes 835592 | tf_op jit(solution)/shard_map/ppermute | solution.py:59
  85.0 3.1 %attend.7 = (bf16[544,256]{1,0:T(8,128)(2,1)S(1)}, bf16[544,256]{1,0:T(8,128)(2,1)S(1)}) custom-call(s32[32,32]{1,0:T(8,128)S(1)} %copy-done.4, bf16[2,256,512]{2,1,0:T(8,128)(2,1)S(1)} %pad_maximum_fusion.refs_1_, bf16[2,2,2,2,128,128]{5,4,3,2,1,0:T(8,128)(2,1)S(1)} %pad_maximum_fusion.1.refs_3_.refs_2_, ...), custom_call_target="tpu_custom_call" | custom-call | flops 2000000000 | bytes 8388608 | tf_op jit(solution)/shard_map/attend/pallas_call | solution.py:347
  90.4 4.4 %collective-permute-done.23.refs_5_ = bf16[544,256]{1,0:T(8,128)(2,1)S(1)} collective-permute-done((bf16[544,256]{1,0:T(8,128)(2,1)S(1)}, bf16[544,256]{1,0:T(8,128)(2,1)S(1)}, u32[]{:S(2)}, u32[]{:S(2)}) %collective-permute-start.23) | collective-permute-done | bytes 278560 | tf_op jit(solution)/shard_map/ppermute | solution.py:59
  (52 shorter events, 17.3 us)
Async XLA Ops:
  2.6 14.4 %collective-permute-start.4 = (bf16[256,1024]{1,0:T(8,128)(2,1)}, bf16[256,1024]{1,0:T(8,128)(2,1)S(1)}, u32[]{:S(2)}, u32[]{:S(2)}) collective-permute-start(bf16[256,1024]{1,0:T(8,128)(2,1)} %bitcast.8), channel_id=1, source_target_pairs={{0,3},{1,0},{2,1},{3,2},{4,7},{5,4},{6,5},{7,6},{8,11},{9,8},{10,9... | collective-permute-start | bytes 1572872 | tf_op jit(solution)/shard_map/ppermute | solution.py:59
  5.4 15.0 %collective-permute-start.6 = (bf16[256,1024]{1,0:T(8,128)(2,1)}, bf16[256,1024]{1,0:T(8,128)(2,1)S(1)}, u32[]{:S(2)}, u32[]{:S(2)}) collective-permute-start(bf16[256,1024]{1,0:T(8,128)(2,1)} %bitcast.9), channel_id=1, source_target_pairs={{0,1},{1,2},{2,3},{3,0},{4,5},{5,6},{6,7},{7,4},{8,9},{9,10},{10,1... | collective-permute-start | bytes 1572872 | tf_op jit(solution)/shard_map/ppermute | solution.py:59
  5.5 15.0 %collective-permute-start.3 = (bf16[2,256,512]{2,1,0:T(8,128)(2,1)S(1)}, bf16[2,256,512]{2,1,0:T(8,128)(2,1)S(1)}, u32[]{:S(2)}, u32[]{:S(2)}) collective-permute-start(bf16[2,256,512]{2,1,0:T(8,128)(2,1)S(1)} %pad_maximum_fusion.refs_1_), channel_id=1, source_target_pairs={{0,16},{1,17},{2,18},{3,19},{4,68},{5,69},{6,70},{7,71},{8,24},{9,... | collective-permute-start | bytes 1572872 | tf_op jit(solution)/shard_map/ppermute | solution.py:59
  8.3 14.9 %collective-permute-start.2 = (bf16[2,256,512]{2,1,0:T(8,128)(2,1)S(1)}, bf16[2,256,512]{2,1,0:T(8,128)(2,1)S(1)}, u32[]{:S(2)}, u32[]{:S(2)}) collective-permute-start(bf16[2,256,512]{2,1,0:T(8,128)(2,1)S(1)} %pad_maximum_fusion.refs_1_), channel_id=1, source_target_pairs={{0,24},{1,25},{2,26},{3,27},{4,100},{5,101},{6,102},{7,103},{8,0},... | collective-permute-start | bytes 1572872 | tf_op jit(solution)/shard_map/ppermute | solution.py:59
  9.1 14.0 %collective-permute-start.1 = (bf16[2,256,512]{2,1,0:T(8,128)(2,1)S(1)}, bf16[2,256,512]{2,1,0:T(8,128)(2,1)S(1)}, u32[]{:S(2)}, u32[]{:S(2)}) collective-permute-start(bf16[2,256,512]{2,1,0:T(8,128)(2,1)S(1)} %pad_maximum_fusion.refs_1_), channel_id=1, source_target_pairs={{0,8},{1,9},{2,10},{3,11},{4,36},{5,37},{6,38},{7,39},{8,16},{9,17... | collective-permute-start | bytes 1572872 | tf_op jit(solution)/shard_map/ppermute | solution.py:59
  17.0 15.9 %collective-permute-start.5 = (bf16[128,1024]{1,0:T(8,128)(2,1)S(1)}, bf16[128,1024]{1,0:T(8,128)(2,1)S(1)}, u32[]{:S(2)}, u32[]{:S(2)}) collective-permute-start(bf16[128,1024]{1,0:T(8,128)(2,1)S(1)} %slice.8), channel_id=1, source_target_pairs={{0,3},{1,0},{2,1},{3,2},{4,7},{5,4},{6,5},{7,6},{8,11},{9,8},{10,9... | collective-permute-start | bytes 786440 | tf_op jit(solution)/shard_map/ppermute | solution.py:59
  20.4 12.5 %collective-permute-start.7 = (bf16[128,1024]{1,0:T(8,128)(2,1)S(1)}, bf16[128,1024]{1,0:T(8,128)(2,1)S(1)}, u32[]{:S(2)}, u32[]{:S(2)}) collective-permute-start(bf16[128,1024]{1,0:T(8,128)(2,1)S(1)} %slice.9), channel_id=1, source_target_pairs={{0,1},{1,2},{2,3},{3,0},{4,5},{5,6},{6,7},{7,4},{8,9},{9,10},{10,1... | collective-permute-start | bytes 786440 | tf_op jit(solution)/shard_map/ppermute | solution.py:59
  20.5 12.4 %collective-permute-start.9 = (bf16[1024]{0:T(1024)(128)(2,1)}, bf16[1024]{0:T(1024)(128)(2,1)S(1)}, u32[]{:S(2)}, u32[]{:S(2)}) collective-permute-start(bf16[1024]{0:T(1024)(128)(2,1)} %refs_5_.1), channel_id=1, source_target_pairs={{0,3},{1,0},{2,1},{3,2},{4,7},{5,4},{6,5},{7,6},{8,11},{9,8},{10,9... | collective-permute-start | bytes 6152 | tf_op jit(solution)/shard_map/ppermute | solution.py:59
  23.2 9.7 %collective-permute-start.8 = (bf16[1024]{0:T(1024)(128)(2,1)}, bf16[1024]{0:T(1024)(128)(2,1)S(1)}, u32[]{:S(2)}, u32[]{:S(2)}) collective-permute-start(bf16[1024]{0:T(1024)(128)(2,1)} %refs_5_.1), channel_id=1, source_target_pairs={{0,1},{1,2},{2,3},{3,0},{4,5},{5,6},{6,7},{7,4},{8,9},{9,10},{10,1... | collective-permute-start | bytes 6152 | tf_op jit(solution)/shard_map/ppermute | solution.py:59
  23.2 9.7 %collective-permute-start.10 = (bf16[1024]{0:T(1024)(128)(2,1)}, bf16[1024]{0:T(1024)(128)(2,1)S(1)}, u32[]{:S(2)}, u32[]{:S(2)}) collective-permute-start(bf16[1024]{0:T(1024)(128)(2,1)} %refs_5_.1), channel_id=1, source_target_pairs={{0,2},{1,3},{2,0},{3,1},{4,6},{5,7},{6,4},{7,5},{8,10},{9,11},{10,... | collective-permute-start | bytes 6152 | tf_op jit(solution)/shard_map/ppermute | solution.py:59
  36.3 4.6 %collective-permute-start.15 = (bf16[2,2,2,128,128]{4,3,2,1,0:T(8,128)(2,1)S(1)}, bf16[2,2,2,128,128]{4,3,2,1,0:T(8,128)(2,1)S(1)}, u32[]{:S(2)}, u32[]{:S(2)}) collective-permute-start(bf16[2,2,2,128,128]{4,3,2,1,0:T(8,128)(2,1)S(1)} %get-tuple-element.38), channel_id=1, source_target_pairs={{0,4},{1,5},{2,6},{3,7},{4,0},{5,1},{6,2},{7,3},{8,12},{9,13},{10,... | collective-permute-start | bytes 786440 | tf_op jit(solution)/shard_map/ppermute | solution.py:59
  40.9 12.0 %collective-permute-start.18 = (bf16[2,2,2,2,128,128]{5,4,3,2,1,0:T(8,128)(2,1)S(1)}, bf16[2,2,2,2,128,128]{5,4,3,2,1,0:T(8,128)(2,1)S(1)}, u32[]{:S(2)}, u32[]{:S(2)}) collective-permute-start(bf16[2,2,2,2,128,128]{5,4,3,2,1,0:T(8,128)(2,1)S(1)} %pad_maximum_fusion.2.refs_5_), channel_id=1, source_target_pairs={{0,64},{1,65},{2,66},{3,67},{4,20},{5,21},{6,22},{7,23},{8,72},{9,... | collective-permute-start | bytes 1572872 | tf_op jit(solution)/shard_map/ppermute | solution.py:59
  42.7 13.7 %collective-permute-start.17 = (bf16[2,2,2,2,128,128]{5,4,3,2,1,0:T(8,128)(2,1)S(1)}, bf16[2,2,2,2,128,128]{5,4,3,2,1,0:T(8,128)(2,1)S(1)}, u32[]{:S(2)}, u32[]{:S(2)}) collective-permute-start(bf16[2,2,2,2,128,128]{5,4,3,2,1,0:T(8,128)(2,1)S(1)} %pad_maximum_fusion.2.refs_5_), channel_id=1, source_target_pairs={{0,96},{1,97},{2,98},{3,99},{4,28},{5,29},{6,30},{7,31},{8,104},{9... | collective-permute-start | bytes 1572872 | tf_op jit(solution)/shard_map/ppermute | solution.py:59
  43.6 12.8 %collective-permute-start.16 = (bf16[2,2,2,2,128,128]{5,4,3,2,1,0:T(8,128)(2,1)S(1)}, bf16[2,2,2,2,128,128]{5,4,3,2,1,0:T(8,128)(2,1)S(1)}, u32[]{:S(2)}, u32[]{:S(2)}) collective-permute-start(bf16[2,2,2,2,128,128]{5,4,3,2,1,0:T(8,128)(2,1)S(1)} %pad_maximum_fusion.2.refs_5_), channel_id=1, source_target_pairs={{0,32},{1,33},{2,34},{3,35},{4,12},{5,13},{6,14},{7,15},{8,40},{9,... | collective-permute-start | bytes 1572872 | tf_op jit(solution)/shard_map/ppermute | solution.py:59
  50.2 15.1 %collective-permute-start.14 = (bf16[2,2,2,2,128,128]{5,4,3,2,1,0:T(8,128)(2,1)S(1)}, bf16[2,2,2,2,128,128]{5,4,3,2,1,0:T(8,128)(2,1)S(1)}, u32[]{:S(2)}, u32[]{:S(2)}) collective-permute-start(bf16[2,2,2,2,128,128]{5,4,3,2,1,0:T(8,128)(2,1)S(1)} %pad_maximum_fusion.1.refs_3_.refs_2_), channel_id=1, source_target_pairs={{0,64},{1,65},{2,66},{3,67},{4,20},{5,21},{6,22},{7,23},{8,72},{9,... | collective-permute-start | bytes 1572872 | tf_op jit(solution)/shard_map/ppermute | solution.py:59
  52.0 15.7 %collective-permute-start.13 = (bf16[2,2,2,2,128,128]{5,4,3,2,1,0:T(8,128)(2,1)S(1)}, bf16[2,2,2,2,128,128]{5,4,3,2,1,0:T(8,128)(2,1)S(1)}, u32[]{:S(2)}, u32[]{:S(2)}) collective-permute-start(bf16[2,2,2,2,128,128]{5,4,3,2,1,0:T(8,128)(2,1)S(1)} %pad_maximum_fusion.1.refs_3_.refs_2_), channel_id=1, source_target_pairs={{0,96},{1,97},{2,98},{3,99},{4,28},{5,29},{6,30},{7,31},{8,104},{9... | collective-permute-start | bytes 1572872 | tf_op jit(solution)/shard_map/ppermute | solution.py:59
  52.9 14.8 %collective-permute-start.12 = (bf16[2,2,2,2,128,128]{5,4,3,2,1,0:T(8,128)(2,1)S(1)}, bf16[2,2,2,2,128,128]{5,4,3,2,1,0:T(8,128)(2,1)S(1)}, u32[]{:S(2)}, u32[]{:S(2)}) collective-permute-start(bf16[2,2,2,2,128,128]{5,4,3,2,1,0:T(8,128)(2,1)S(1)} %pad_maximum_fusion.1.refs_3_.refs_2_), channel_id=1, source_target_pairs={{0,32},{1,33},{2,34},{3,35},{4,12},{5,13},{6,14},{7,15},{8,40},{9,... | collective-permute-start | bytes 1572872 | tf_op jit(solution)/shard_map/ppermute | solution.py:59
  70.9 17.3 %collective-permute-start.21 = (bf16[544,256]{1,0:T(8,128)(2,1)S(1)}, bf16[544,256]{1,0:T(8,128)(2,1)S(1)}, u32[]{:S(2)}, u32[]{:S(2)}) collective-permute-start(bf16[544,256]{1,0:T(8,128)(2,1)S(1)} %get-tuple-element.43), channel_id=1, source_target_pairs={{0,8},{1,9},{2,10},{3,11},{4,36},{5,37},{6,38},{7,39},{8,16},{9,17... | collective-permute-start | bytes 835592 | tf_op jit(solution)/shard_map/ppermute | solution.py:59
  72.4 16.7 %collective-permute-start.24 = (bf16[544,256]{1,0:T(8,128)(2,1)S(1)}, bf16[544,256]{1,0:T(8,128)(2,1)S(1)}, u32[]{:S(2)}, u32[]{:S(2)}) collective-permute-start(bf16[544,256]{1,0:T(8,128)(2,1)S(1)} %get-tuple-element.47), channel_id=1, source_target_pairs={{0,12},{1,13},{2,14},{3,15},{4,32},{5,33},{6,34},{7,35},{8,20},{9,... | collective-permute-start | bytes 835592 | tf_op jit(solution)/shard_map/ppermute | solution.py:59
  78.7 10.6 %collective-permute-start.19 = (bf16[544,256]{1,0:T(8,128)(2,1)S(1)}, bf16[544,256]{1,0:T(8,128)(2,1)S(1)}, u32[]{:S(2)}, u32[]{:S(2)}) collective-permute-start(bf16[544,256]{1,0:T(8,128)(2,1)S(1)} %get-tuple-element.41), channel_id=1, source_target_pairs={{0,16},{1,17},{2,18},{3,19},{4,68},{5,69},{6,70},{7,71},{8,24},{9,... | collective-permute-start | bytes 835592 | tf_op jit(solution)/shard_map/ppermute | solution.py:59
  81.6 7.7 %collective-permute-start.20 = (bf16[544,256]{1,0:T(8,128)(2,1)S(1)}, bf16[544,256]{1,0:T(8,128)(2,1)S(1)}, u32[]{:S(2)}, u32[]{:S(2)}) collective-permute-start(bf16[544,256]{1,0:T(8,128)(2,1)S(1)} %get-tuple-element.42), channel_id=1, source_target_pairs={{0,24},{1,25},{2,26},{3,27},{4,100},{5,101},{6,102},{7,103},{8,0},... | collective-permute-start | bytes 835592 | tf_op jit(solution)/shard_map/ppermute | solution.py:59
  82.9 7.5 %collective-permute-start.22 = (bf16[544,256]{1,0:T(8,128)(2,1)S(1)}, bf16[544,256]{1,0:T(8,128)(2,1)S(1)}, u32[]{:S(2)}, u32[]{:S(2)}) collective-permute-start(bf16[544,256]{1,0:T(8,128)(2,1)S(1)} %get-tuple-element.45), channel_id=1, source_target_pairs={{0,20},{1,21},{2,22},{3,23},{4,64},{5,65},{6,66},{7,67},{8,28},{9,... | collective-permute-start | bytes 835592 | tf_op jit(solution)/shard_map/ppermute | solution.py:59
  88.1 6.6 %collective-permute-start.23 = (bf16[544,256]{1,0:T(8,128)(2,1)S(1)}, bf16[544,256]{1,0:T(8,128)(2,1)S(1)}, u32[]{:S(2)}, u32[]{:S(2)}) collective-permute-start(bf16[544,256]{1,0:T(8,128)(2,1)S(1)} %get-tuple-element.46), channel_id=1, source_target_pairs={{0,28},{1,29},{2,30},{3,31},{4,96},{5,97},{6,98},{7,99},{8,4},{9,5... | collective-permute-start | bytes 835592 | tf_op jit(solution)/shard_map/ppermute | solution.py:59
  89.1 5.7 %collective-permute-start.25 = (bf16[544,256]{1,0:T(8,128)(2,1)S(1)}, bf16[544,256]{1,0:T(8,128)(2,1)S(1)}, u32[]{:S(2)}, u32[]{:S(2)}) collective-permute-start(bf16[544,256]{1,0:T(8,128)(2,1)S(1)} %get-tuple-element.48), channel_id=1, source_target_pairs={{0,4},{1,5},{2,6},{3,7},{4,0},{5,1},{6,2},{7,3},{8,12},{9,13},{10,... | collective-permute-start | bytes 835592 | tf_op jit(solution)/shard_map/ppermute | solution.py:59
  (7 other events, 55.4 us)

commit v3 on v2

--- a/solution.py
+++ b/solution.py
@@ -95,7 +95,7 @@
         in_specs=[anywhere()] * 2,
         out_specs=(vmem(),) * 2,
         scratch_shapes=[pltpu.SemaphoreType.DMA((2,))],
-        compiler_params=pltpu.CompilerParams(vmem_limit_bytes=20 * MIB),
+        compiler_params=pltpu.CompilerParams(vmem_limit_bytes=2 * MIB),
         cost_estimate=pl.CostEstimate(flops=0, bytes_accessed=1024, transcendentals=0),
         name="preload",
     )(key_weight, value_weight)
@@ -103,24 +103,26 @@
 
 def normalise(x_refs, gain_refs, normed):
     width = x_refs[0].shape[1]
+    gains = [gain_refs[0][...].reshape(1, width).astype(F32)]
+    gains += [far[BLOCK:, :].astype(F32)[0:1] for far in x_refs[3:]]
+    gains += [gain_refs[1][...].reshape(1, width).astype(F32)]
     for block in range(2):
         rows = pl.ds(block * BLOCK, BLOCK)
-        parts = [x_ref[rows, :] for x_ref in x_refs[:3]] + [x_refs[3 + block][...]]
+        parts = [x_ref[rows, :] for x_ref in x_refs[:3]] + [x_refs[3 + block][:BLOCK, :]]
         total = jnp.zeros((BLOCK, 1), F32)
         for part in parts:
             floats = part.astype(F32)
             total += jnp.sum(floats * floats, axis=-1, keepdims=True)
         scale = lax.rsqrt(total * (1.0 / (4 * width)) + 1e-06)
         for slot, part in enumerate(parts):
-            gain = gain_refs[slot][...].reshape(1, width).astype(F32)
-            normed[slot, rows, :] = (part.astype(F32) * scale * gain).astype(BF16)
+            normed[slot, rows, :] = (part.astype(F32) * scale * gains[slot]).astype(BF16)
 
 
 def project_kernel(part, *refs):
     refs = list(refs)
     if part == 0:
         x_refs = [refs.pop(0) for _ in range(5)]
-        gain_refs = [refs.pop(0) for _ in range(4)]
+        gain_refs = [refs.pop(0) for _ in range(2)]
     else:
         normed = refs.pop(0)
     weight_refs = [refs.pop(0) for _ in range(2)]
@@ -162,7 +164,7 @@
         out_shape=tuple(shapes),
         in_specs=[vmem()] * (len(inputs) + 2),
         out_specs=(vmem(),) * len(shapes),
-        compiler_params=pltpu.CompilerParams(vmem_limit_bytes=28 * MIB),
+        compiler_params=pltpu.CompilerParams(vmem_limit_bytes=12 * MIB),
         cost_estimate=pl.CostEstimate(flops=0, bytes_accessed=1024, transcendentals=0),
         name="project",
     )(*inputs, key_weight, value_weight)
@@ -426,17 +428,28 @@
     core = place()[2]
     own = block_states.reshape(ROWS, block_states.shape[2])
     left, right = send(own, along_y(1)), send(own, along_y(-1))
-    gains = gather(norm_gain, along_y)
-    mine = lax.dynamic_slice_in_dim(queries, core * HALF, HALF, 1)
-    away = lax.dynamic_slice_in_dim(queries, (1 - core) * HALF, HALF, 1)
-    slots_q = gather(both_cores(mine, away), q_ring)
+    far_gain = send(norm_gain, along_y(2))
+    other = send(queries, CORE_SWAP)
+    halves = [lax.dynamic_slice_in_dim(each, core * HALF, HALF, 1)[None] for each in (queries, other)]
+    q_pair = jnp.concatenate(halves, axis=0)
+    q_far, q_right = send(q_pair, q_ring(2)), send(q_pair, q_ring(-1))
+    gain_rows = jnp.broadcast_to(norm_gain[None], (16, norm_gain.shape[0]))
     key_weight, value_weight = preload(key_weight, value_weight)
-    far = [send(left[:BLOCK], along_y(1)), send(right[BLOCK:], along_y(-1))]
-    *slots_q, far[1] = lax.optimization_barrier((*slots_q, far[1]))
-    inputs = [own, left, right, *far, *gains]
+    left, right, key_weight, value_weight = lax.optimization_barrier(
+        (left, right, key_weight, value_weight)
+    )
+    far = [
+        send(jnp.concatenate([left[:BLOCK], gain_rows], axis=0), along_y(1)),
+        send(jnp.concatenate([right[BLOCK:], gain_rows], axis=0), along_y(-1)),
+    ]
+    q_left = send(lax.optimization_barrier((q_pair, left))[0], q_ring(1))
+    q_far, q_right, far[0] = lax.optimization_barrier((q_far, q_right, far[0]))
+    inputs = [own, left, right, *far, norm_gain, far_gain]
     *ready, normed = project(0, inputs, key_weight, value_weight)
     kv = gather(both_cores(*ready), kv_ring)
+    normed, q_left = lax.optimization_barrier((normed, q_left))
     kv_late = gather(both_cores(*project(1, [normed], key_weight, value_weight)), kv_ring)
+    slots_q = [q_pair, q_left, q_right, q_far]
     early = attend(0, wanted, slots_q, kv, (0, 1, 2, 3))
     mine, away = [], []
     for slots in ((3, 1), (2,), (0,)):

time: 96.7 us -> 91 us (0.941)
  waiting for transfers between devices: 20.4 us -> 13.3 us
    ppermute x26 -> x24, waiting for transfers between devices: 20.4 us -> 13.3 us  [send(): return lax.ppermute(array, AXES, pairs)]
    ppermute x26 -> x24, starting transfers between devices: 39.2 us -> 40 us  [send(): return lax.ppermute(array, AXES, pairs)]
  transfers between devices with their start and end apart: 26 -> 24, of which waited for: 7 -> 7; matrix products, arithmetic and copies ran while one was open for 0% -> 1% of each run, Pallas kernels for 21% -> 25%
where the time goes in v3:
time: 91 us; the launch traced here: 90.5 us
  starting transfers between devices  40 us (44%)
  Pallas kernels  28.9 us (32%)
  waiting for transfers between devices  13.3 us (15%)
  local copies, waits for them, and re-layouts  7.82 us (9%)
    ppermute x24, starting transfers between devices, send(): return lax.ppermute(array, AXES, pairs)  40 us
    pallas_call x4, Pallas kernels, attend(): pl.pallas_call(functools.partial(attend_kernel, part, slots), out_shape=o...  20.5 us
    ppermute x24, waiting for transfers between devices, send(): return lax.ppermute(array, AXES, pairs)  13.3 us
    unnamed x10, local copies, waits for them, and re-layouts  6.78 us
    pallas_call x2, Pallas kernels, project(): pl.pallas_call(functools.partial(project_kernel, part), out_shape=tuple(s...  5.86 us
  transfers between devices with their start and end apart: 24, of which 7 were waited for; matrix products, arithmetic and copies ran while one was open for 1% of the time, Pallas kernels for 25%

profile of v3, /device:TPU:1, one launch (start us, length us, event | category | flops | bytes accessed | tf_op | source)
XLA Modules:
  0.0 90.5 jit_solution(18042531490851980507)
XLA Ops:
  2.8 1.4 %collective-permute-start.4 = (bf16[256,1024]{1,0:T(8,128)(2,1)}, bf16[256,1024]{1,0:T(8,128)(2,1)S(1)}, u32[]{:S(2)}, u32[]{:S(2)}) collective-permute-start(bf16[256,1024]{1,0:T(8,128)(2,1)} %bitcast.10), channel_id=1, source_target_pairs={{0,3},{1,0},{2,1},{3,2},{4,7},{5,4},{6,5},{7,6},{8,11},{9,8},{10,9... | collective-permute-start | bytes 1572872 | tf_op jit(solution)/shard_map/ppermute | solution.py:59
  5.3 2.8 %collective-permute-start.1 = (bf16[2,256,512]{2,1,0:T(8,128)(2,1)S(1)}, bf16[2,256,512]{2,1,0:T(8,128)(2,1)S(1)}, u32[]{:S(2)}, u32[]{:S(2)}) collective-permute-start(bf16[2,256,512]{2,1,0:T(8,128)(2,1)S(1)} %pad_maximum_fusion.refs_1_), channel_id=1, source_target_pairs={{0,16},{1,17},{2,18},{3,19},{4,68},{5,69},{6,70},{7,71},{8,24},{9,... | collective-permute-start | bytes 1572872 | tf_op jit(solution)/shard_map/ppermute | solution.py:59
  9.0 3.4 %copy-done = bf16[4096,1024]{1,0:T(8,128)(2,1)S(1)} copy-done((bf16[4096,1024]{1,0:T(8,128)(2,1)S(1)}, bf16[4096,1024]{1,0:T(8,128)(2,1)}, u32[]{:S(2)}) %copy-start) | copy-done | bytes 8388632
  12.4 3.4 %copy-done.1 = bf16[4096,1024]{1,0:T(8,128)(2,1)S(1)} copy-done((bf16[4096,1024]{1,0:T(8,128)(2,1)S(1)}, bf16[4096,1024]{1,0:T(8,128)(2,1)}, u32[]{:S(2)}) %copy-start.1) | copy-done | bytes 8388632
  17.7 2.1 %collective-permute-start.6 = (bf16[144,1024]{1,0:T(8,128)(2,1)S(1)}, bf16[144,1024]{1,0:T(8,128)(2,1)S(1)}, u32[]{:S(2)}, u32[]{:S(2)}) collective-permute-start(bf16[144,1024]{1,0:T(8,128)(2,1)S(1)} %get-tuple-element.59), channel_id=1, source_target_pairs={{0,3},{1,0},{2,1},{3,2},{4,7},{5,4},{6,5},{7,6},{8,11},{9,8},{10,9... | collective-permute-start | bytes 884744 | tf_op jit(solution)/shard_map/ppermute | solution.py:59
  20.5 4.8 %collective-permute-done.5.refs_3_ = bf16[144,1024]{1,0:T(8,128)(2,1)S(1)} collective-permute-done((bf16[144,1024]{1,0:T(8,128)(2,1)S(1)}, bf16[144,1024]{1,0:T(8,128)(2,1)S(1)}, u32[]{:S(2)}, u32[]{:S(2)}) %collective-permute-start.5) | collective-permute-done | bytes 294944 | tf_op jit(solution)/shard_map/ppermute | solution.py:59
  26.3 3.4 %project.2 = (bf16[2,2,2,128,128]{4,3,2,1,0:T(8,128)(2,1)S(1)}, bf16[2,2,2,128,128]{4,3,2,1,0:T(8,128)(2,1)S(1)}, bf16[4,256,1024]{2,1,0:T(8,128)(2,1)S(1)}) custom-call(bf16[256,1024]{1,0:T(8,128)(2,1)S(1)} %bitcast.11, bf16[256,1024]{1,0:T(8,128)(2,1)S(1)} %collective-permute-done.3.refs_1_, bf16[256,1024]{1,0:T(8,128)(2,1)S(1)} %collective-permute-done.4.refs_2_, ...), custom_call_target="tpu_custom_call" | custom-call | bytes 1024 | tf_op jit(solution)/shard_map/project/pallas_call | solution.py:162
  29.6 3.6 %collective-permute-start.13 = (bf16[2,2,2,128,128]{4,3,2,1,0:T(8,128)(2,1)S(1)}, bf16[2,2,2,128,128]{4,3,2,1,0:T(8,128)(2,1)S(1)}, u32[]{:S(2)}, u32[]{:S(2)}) collective-permute-start(bf16[2,2,2,128,128]{4,3,2,1,0:T(8,128)(2,1)S(1)} %get-tuple-element.48), channel_id=1, source_target_pairs={{0,4},{1,5},{2,6},{3,7},{4,0},{5,1},{6,2},{7,3},{8,12},{9,13},{10,... | collective-permute-start | bytes 786440 | tf_op jit(solution)/shard_map/ppermute | solution.py:59
  34.4 1.7 %collective-permute-start.14 = (bf16[2,2,2,2,128,128]{5,4,3,2,1,0:T(8,128)(2,1)S(1)}, bf16[2,2,2,2,128,128]{5,4,3,2,1,0:T(8,128)(2,1)S(1)}, u32[]{:S(2)}, u32[]{:S(2)}) collective-permute-start(bf16[2,2,2,2,128,128]{5,4,3,2,1,0:T(8,128)(2,1)S(1)} %pad_maximum_fusion.2.refs_5_), channel_id=1, source_target_pairs={{0,32},{1,33},{2,34},{3,35},{4,12},{5,13},{6,14},{7,15},{8,40},{9,... | collective-permute-start | bytes 1572872 | tf_op jit(solution)/shard_map/ppermute | solution.py:59
  37.2 2.1 %collective-permute-start.16 = (bf16[2,2,2,2,128,128]{5,4,3,2,1,0:T(8,128)(2,1)S(1)}, bf16[2,2,2,2,128,128]{5,4,3,2,1,0:T(8,128)(2,1)S(1)}, u32[]{:S(2)}, u32[]{:S(2)}) collective-permute-start(bf16[2,2,2,2,128,128]{5,4,3,2,1,0:T(8,128)(2,1)S(1)} %pad_maximum_fusion.2.refs_5_), channel_id=1, source_target_pairs={{0,64},{1,65},{2,66},{3,67},{4,20},{5,21},{6,22},{7,23},{8,72},{9,... | collective-permute-start | bytes 1572872 | tf_op jit(solution)/shard_map/ppermute | solution.py:59
  39.3 2.5 %project.3 = (bf16[2,2,2,128,128]{4,3,2,1,0:T(8,128)(2,1)S(1)}, bf16[2,2,2,128,128]{4,3,2,1,0:T(8,128)(2,1)S(1)}) custom-call(bf16[4,256,1024]{2,1,0:T(8,128)(2,1)S(1)} %get-tuple-element.43.refs_0_, bf16[4096,1024]{1,0:T(8,128)(2,1)S(1)} %get-tuple-element.38.refs_7_.refs_1_, bf16[4096,1024]{1,0:T(8,128)(2,1)S(1)} %get-tuple-element.39.refs_8_.refs_2_), custom_call_target="tpu_custom_call" | custom-call | bytes 1024 | tf_op jit(solution)/shard_map/project/pallas_call | solution.py:162
  43.4 1.7 %collective-permute-start.10 = (bf16[2,2,2,2,128,128]{5,4,3,2,1,0:T(8,128)(2,1)S(1)}, bf16[2,2,2,2,128,128]{5,4,3,2,1,0:T(8,128)(2,1)S(1)}, u32[]{:S(2)}, u32[]{:S(2)}) collective-permute-start(bf16[2,2,2,2,128,128]{5,4,3,2,1,0:T(8,128)(2,1)S(1)} %pad_maximum_fusion.1.refs_3_.refs_2_), channel_id=1, source_target_pairs={{0,32},{1,33},{2,34},{3,35},{4,12},{5,13},{6,14},{7,15},{8,40},{9,... | collective-permute-start | bytes 1572872 | tf_op jit(solution)/shard_map/ppermute | solution.py:59
  46.3 5.5 %collective-permute-start.12 = (bf16[2,2,2,2,128,128]{5,4,3,2,1,0:T(8,128)(2,1)S(1)}, bf16[2,2,2,2,128,128]{5,4,3,2,1,0:T(8,128)(2,1)S(1)}, u32[]{:S(2)}, u32[]{:S(2)}) collective-permute-start(bf16[2,2,2,2,128,128]{5,4,3,2,1,0:T(8,128)(2,1)S(1)} %pad_maximum_fusion.1.refs_3_.refs_2_), channel_id=1, source_target_pairs={{0,64},{1,65},{2,66},{3,67},{4,20},{5,21},{6,22},{7,23},{8,72},{9,... | collective-permute-start | bytes 1572872 | tf_op jit(solution)/shard_map/ppermute | solution.py:59
  51.8 9.1 %attend.4 = (bf16[8,256,256]{2,1,0:T(8,128)(2,1)S(1)}, f32[8,8,256]{2,1,0:T(8,128)S(1)}) custom-call(s32[32,32]{1,0:T(8,128)S(1)} %copy-done.4, bf16[2,256,512]{2,1,0:T(8,128)(2,1)S(1)} %pad_maximum_fusion.refs_1_, bf16[2,256,512]{2,1,0:T(8,128)(2,1)S(1)} %collective-permute-done.8.refs_2_, bf16[2,256,512]{2,1,0:T(8,128)(2,1)S(1)} %collective-permute-done.2.refs_3_.refs_1_, ...), custom_call_target="tpu_custom_call" | custom-call | flops 8000000000 | bytes 8388608 | tf_op jit(solution)/shard_map/attend/pallas_call | solution.py:349
  60.9 1.5 %collective-permute-done.12.refs_6_.refs_5_ = bf16[2,2,2,2,128,128]{5,4,3,2,1,0:T(8,128)(2,1)S(1)} collective-permute-done((bf16[2,2,2,2,128,128]{5,4,3,2,1,0:T(8,128)(2,1)S(1)}, bf16[2,2,2,2,128,128]{5,4,3,2,1,0:T(8,128)(2,1)S(1)}, u32[]{:S(2)}, u32[]{:S(2)}) %collective-permute-start.12) | collective-permute-done | bytes 524320 | tf_op jit(solution)/shard_map/ppermute | solution.py:59
  62.4 5.1 %attend.5 = (bf16[544,256]{1,0:T(8,128)(2,1)S(1)}, bf16[544,256]{1,0:T(8,128)(2,1)S(1)}, bf16[544,256]{1,0:T(8,128)(2,1)S(1)}, bf16[544,256]{1,0:T(8,128)(2,1)S(1)}) custom-call(s32[32,32]{1,0:T(8,128)S(1)} %copy-done.4, bf16[2,256,512]{2,1,0:T(8,128)(2,1)S(1)} %collective-permute-done.1.refs_4_.refs_1_, ...), custom_call_target="tpu_custom_call" | custom-call | flops 4000000000 | bytes 8388608 | tf_op jit(solution)/shard_map/attend/pallas_call | solution.py:349
  67.5 2.6 %collective-permute-start.17 = (bf16[544,256]{1,0:T(8,128)(2,1)S(1)}, bf16[544,256]{1,0:T(8,128)(2,1)S(1)}, u32[]{:S(2)}, u32[]{:S(2)}) collective-permute-start(bf16[544,256]{1,0:T(8,128)(2,1)S(1)} %get-tuple-element.51), channel_id=1, source_target_pairs={{0,16},{1,17},{2,18},{3,19},{4,68},{5,69},{6,70},{7,71},{8,24},{9,... | collective-permute-start | bytes 835592 | tf_op jit(solution)/shard_map/ppermute | solution.py:59
  70.7 3.3 %attend.6 = (bf16[544,256]{1,0:T(8,128)(2,1)S(1)}, bf16[544,256]{1,0:T(8,128)(2,1)S(1)}) custom-call(s32[32,32]{1,0:T(8,128)S(1)} %copy-done.4, bf16[2,256,512]{2,1,0:T(8,128)(2,1)S(1)} %collective-permute-done.2.refs_3_.refs_1_, bf16[2,2,2,2,128,128]{5,4,3,2,1,0:T(8,128)(2,1)S(1)} %pad_maximum_fusion.1.refs_3_.refs_2_, ...), custom_call_target="tpu_custom_call" | custom-call | flops 2000000000 | bytes 8388608 | tf_op jit(solution)/shard_map/attend/pallas_call | solution.py:349
  74.5 2.4 %collective-permute-start.20 = (bf16[544,256]{1,0:T(8,128)(2,1)S(1)}, bf16[544,256]{1,0:T(8,128)(2,1)S(1)}, u32[]{:S(2)}, u32[]{:S(2)}) collective-permute-start(bf16[544,256]{1,0:T(8,128)(2,1)S(1)} %get-tuple-element.55), channel_id=1, source_target_pairs={{0,20},{1,21},{2,22},{3,23},{4,64},{5,65},{6,66},{7,67},{8,28},{9,... | collective-permute-start | bytes 835592 | tf_op jit(solution)/shard_map/ppermute | solution.py:59
  77.0 1.5 %collective-permute-start.21 = (bf16[544,256]{1,0:T(8,128)(2,1)S(1)}, bf16[544,256]{1,0:T(8,128)(2,1)S(1)}, u32[]{:S(2)}, u32[]{:S(2)}) collective-permute-start(bf16[544,256]{1,0:T(8,128)(2,1)S(1)} %get-tuple-element.56), channel_id=1, source_target_pairs={{0,28},{1,29},{2,30},{3,31},{4,96},{5,97},{6,98},{7,99},{8,4},{9,5... | collective-permute-start | bytes 835592 | tf_op jit(solution)/shard_map/ppermute | solution.py:59
  78.5 2.9 %attend.7 = (bf16[544,256]{1,0:T(8,128)(2,1)S(1)}, bf16[544,256]{1,0:T(8,128)(2,1)S(1)}) custom-call(s32[32,32]{1,0:T(8,128)S(1)} %copy-done.4, bf16[2,256,512]{2,1,0:T(8,128)(2,1)S(1)} %pad_maximum_fusion.refs_1_, bf16[2,2,2,2,128,128]{5,4,3,2,1,0:T(8,128)(2,1)S(1)} %pad_maximum_fusion.1.refs_3_.refs_2_, ...), custom_call_target="tpu_custom_call" | custom-call | flops 2000000000 | bytes 8388608 | tf_op jit(solution)/shard_map/attend/pallas_call | solution.py:349
  81.4 3.3 %collective-permute-start.22 = (bf16[544,256]{1,0:T(8,128)(2,1)S(1)}, bf16[544,256]{1,0:T(8,128)(2,1)S(1)}, u32[]{:S(2)}, u32[]{:S(2)}) collective-permute-start(bf16[544,256]{1,0:T(8,128)(2,1)S(1)} %get-tuple-element.57), channel_id=1, source_target_pairs={{0,12},{1,13},{2,14},{3,15},{4,32},{5,33},{6,34},{7,35},{8,20},{9,... | collective-permute-start | bytes 835592 | tf_op jit(solution)/shard_map/ppermute | solution.py:59
  85.0 4.0 %collective-permute-done.22.refs_6_ = bf16[544,256]{1,0:T(8,128)(2,1)S(1)} collective-permute-done((bf16[544,256]{1,0:T(8,128)(2,1)S(1)}, bf16[544,256]{1,0:T(8,128)(2,1)S(1)}, u32[]{:S(2)}, u32[]{:S(2)}) %collective-permute-start.22) | collective-permute-done | bytes 278560 | tf_op jit(solution)/shard_map/ppermute | solution.py:59
  89.0 1.5 %merge.1 = bf16[256,1024]{1,0:T(8,128)(2,1)} custom-call(bf16[544,256]{1,0:T(8,128)(2,1)S(1)} %collective-permute-done.17.refs_0_, bf16[544,256]{1,0:T(8,128)(2,1)S(1)} %collective-permute-done.18.refs_1_, bf16[544,256]{1,0:T(8,128)(2,1)S(1)} %collective-permute-done.19.refs_2_, bf16[544,256]{1,0:T(8,128)(2,1)S(1)} %get-tuple-element.54.refs_3_, ...), custom_call_target="tpu_custom_call" | custom-call | tf_op jit(solution)/shard_map/merge/pallas_call | solution.py:411
  (51 shorter events, 14.6 us)
Async XLA Ops:
  0.0 5.2 %collective-permute-start = (bf16[256,1024]{1,0:T(8,128)(2,1)}, bf16[256,1024]{1,0:T(8,128)(2,1)S(1)}, u32[]{:S(2)}, u32[]{:S(2)}) collective-permute-start(bf16[256,1024]{1,0:T(8,128)(2,1)} %param.10), channel_id=1, source_target_pairs={{0,4},{1,5},{2,6},{3,7},{4,0},{5,1},{6,2},{7,3},{8,12},{9,13},{10,... | collective-permute-start | bytes 1572872 | tf_op jit(solution)/shard_map/ppermute | solution.py:59
  1.4 15.5 %collective-permute-start.3 = (bf16[256,1024]{1,0:T(8,128)(2,1)}, bf16[256,1024]{1,0:T(8,128)(2,1)S(1)}, u32[]{:S(2)}, u32[]{:S(2)}) collective-permute-start(bf16[256,1024]{1,0:T(8,128)(2,1)} %bitcast.9), channel_id=1, source_target_pairs={{0,1},{1,2},{2,3},{3,0},{4,5},{5,6},{6,7},{7,4},{8,9},{9,10},{10,1... | collective-permute-start | bytes 1572872 | tf_op jit(solution)/shard_map/ppermute | solution.py:59
  2.8 14.1 %collective-permute-start.4 = (bf16[256,1024]{1,0:T(8,128)(2,1)}, bf16[256,1024]{1,0:T(8,128)(2,1)S(1)}, u32[]{:S(2)}, u32[]{:S(2)}) collective-permute-start(bf16[256,1024]{1,0:T(8,128)(2,1)} %bitcast.10), channel_id=1, source_target_pairs={{0,3},{1,0},{2,1},{3,2},{4,7},{5,4},{6,5},{7,6},{8,11},{9,8},{10,9... | collective-permute-start | bytes 1572872 | tf_op jit(solution)/shard_map/ppermute | solution.py:59
  5.3 20.6 %collective-permute-start.1 = (bf16[2,256,512]{2,1,0:T(8,128)(2,1)S(1)}, bf16[2,256,512]{2,1,0:T(8,128)(2,1)S(1)}, u32[]{:S(2)}, u32[]{:S(2)}) collective-permute-start(bf16[2,256,512]{2,1,0:T(8,128)(2,1)S(1)} %pad_maximum_fusion.refs_1_), channel_id=1, source_target_pairs={{0,16},{1,17},{2,18},{3,19},{4,68},{5,69},{6,70},{7,71},{8,24},{9,... | collective-permute-start | bytes 1572872 | tf_op jit(solution)/shard_map/ppermute | solution.py:59
  8.2 17.7 %collective-permute-start.2 = (bf16[2,256,512]{2,1,0:T(8,128)(2,1)S(1)}, bf16[2,256,512]{2,1,0:T(8,128)(2,1)S(1)}, u32[]{:S(2)}, u32[]{:S(2)}) collective-permute-start(bf16[2,256,512]{2,1,0:T(8,128)(2,1)S(1)} %pad_maximum_fusion.refs_1_), channel_id=1, source_target_pairs={{0,24},{1,25},{2,26},{3,27},{4,100},{5,101},{6,102},{7,103},{8,0},... | collective-permute-start | bytes 1572872 | tf_op jit(solution)/shard_map/ppermute | solution.py:59
  17.1 8.3 %collective-permute-start.5 = (bf16[144,1024]{1,0:T(8,128)(2,1)S(1)}, bf16[144,1024]{1,0:T(8,128)(2,1)S(1)}, u32[]{:S(2)}, u32[]{:S(2)}) collective-permute-start(bf16[144,1024]{1,0:T(8,128)(2,1)S(1)} %get-tuple-element.60), channel_id=1, source_target_pairs={{0,1},{1,2},{2,3},{3,0},{4,5},{5,6},{6,7},{7,4},{8,9},{9,10},{10,1... | collective-permute-start | bytes 884744 | tf_op jit(solution)/shard_map/ppermute | solution.py:59
  17.7 8.5 %collective-permute-start.6 = (bf16[144,1024]{1,0:T(8,128)(2,1)S(1)}, bf16[144,1024]{1,0:T(8,128)(2,1)S(1)}, u32[]{:S(2)}, u32[]{:S(2)}) collective-permute-start(bf16[144,1024]{1,0:T(8,128)(2,1)S(1)} %get-tuple-element.59), channel_id=1, source_target_pairs={{0,3},{1,0},{2,1},{3,2},{4,7},{5,4},{6,5},{7,6},{8,11},{9,8},{10,9... | collective-permute-start | bytes 884744 | tf_op jit(solution)/shard_map/ppermute | solution.py:59
  19.8 6.4 %collective-permute-start.7 = (bf16[1024]{0:T(1024)(128)(2,1)S(1)}, bf16[1024]{0:T(1024)(128)(2,1)S(1)}, u32[]{:S(2)}, u32[]{:S(2)}) collective-permute-start(bf16[1024]{0:T(1024)(128)(2,1)S(1)} %copy-done.3), channel_id=1, source_target_pairs={{0,2},{1,3},{2,0},{3,1},{4,6},{5,7},{6,4},{7,5},{8,10},{9,11},{10,... | collective-permute-start | bytes 6152 | tf_op jit(solution)/shard_map/ppermute | solution.py:59
  25.4 13.9 %collective-permute-start.8 = (bf16[2,256,512]{2,1,0:T(8,128)(2,1)S(1)}, bf16[2,256,512]{2,1,0:T(8,128)(2,1)S(1)}, u32[]{:S(2)}, u32[]{:S(2)}) collective-permute-start(bf16[2,256,512]{2,1,0:T(8,128)(2,1)S(1)} %pad_maximum_fusion.refs_1_), channel_id=1, source_target_pairs={{0,8},{1,9},{2,10},{3,11},{4,36},{5,37},{6,38},{7,39},{8,16},{9,17... | collective-permute-start | bytes 1572872 | tf_op jit(solution)/shard_map/ppermute | solution.py:59
  29.6 4.7 %collective-permute-start.13 = (bf16[2,2,2,128,128]{4,3,2,1,0:T(8,128)(2,1)S(1)}, bf16[2,2,2,128,128]{4,3,2,1,0:T(8,128)(2,1)S(1)}, u32[]{:S(2)}, u32[]{:S(2)}) collective-permute-start(bf16[2,2,2,128,128]{4,3,2,1,0:T(8,128)(2,1)S(1)} %get-tuple-element.48), channel_id=1, source_target_pairs={{0,4},{1,5},{2,6},{3,7},{4,0},{5,1},{6,2},{7,3},{8,12},{9,13},{10,... | collective-permute-start | bytes 786440 | tf_op jit(solution)/shard_map/ppermute | solution.py:59
  34.4 11.8 %collective-permute-start.14 = (bf16[2,2,2,2,128,128]{5,4,3,2,1,0:T(8,128)(2,1)S(1)}, bf16[2,2,2,2,128,128]{5,4,3,2,1,0:T(8,128)(2,1)S(1)}, u32[]{:S(2)}, u32[]{:S(2)}) collective-permute-start(bf16[2,2,2,2,128,128]{5,4,3,2,1,0:T(8,128)(2,1)S(1)} %pad_maximum_fusion.2.refs_5_), channel_id=1, source_target_pairs={{0,32},{1,33},{2,34},{3,35},{4,12},{5,13},{6,14},{7,15},{8,40},{9,... | collective-permute-start | bytes 1572872 | tf_op jit(solution)/shard_map/ppermute | solution.py:59
  36.1 15.6 %collective-permute-start.15 = (bf16[2,2,2,2,128,128]{5,4,3,2,1,0:T(8,128)(2,1)S(1)}, bf16[2,2,2,2,128,128]{5,4,3,2,1,0:T(8,128)(2,1)S(1)}, u32[]{:S(2)}, u32[]{:S(2)}) collective-permute-start(bf16[2,2,2,2,128,128]{5,4,3,2,1,0:T(8,128)(2,1)S(1)} %pad_maximum_fusion.2.refs_5_), channel_id=1, source_target_pairs={{0,96},{1,97},{2,98},{3,99},{4,28},{5,29},{6,30},{7,31},{8,104},{9... | collective-permute-start | bytes 1572872 | tf_op jit(solution)/shard_map/ppermute | solution.py:59
  37.2 14.6 %collective-permute-start.16 = (bf16[2,2,2,2,128,128]{5,4,3,2,1,0:T(8,128)(2,1)S(1)}, bf16[2,2,2,2,128,128]{5,4,3,2,1,0:T(8,128)(2,1)S(1)}, u32[]{:S(2)}, u32[]{:S(2)}) collective-permute-start(bf16[2,2,2,2,128,128]{5,4,3,2,1,0:T(8,128)(2,1)S(1)} %pad_maximum_fusion.2.refs_5_), channel_id=1, source_target_pairs={{0,64},{1,65},{2,66},{3,67},{4,20},{5,21},{6,22},{7,23},{8,72},{9,... | collective-permute-start | bytes 1572872 | tf_op jit(solution)/shard_map/ppermute | solution.py:59
  41.8 1.6 %collective-permute-start.9 = (bf16[2,2,2,128,128]{4,3,2,1,0:T(8,128)(2,1)S(1)}, bf16[2,2,2,128,128]{4,3,2,1,0:T(8,128)(2,1)S(1)}, u32[]{:S(2)}, u32[]{:S(2)}) collective-permute-start(bf16[2,2,2,128,128]{4,3,2,1,0:T(8,128)(2,1)S(1)} %get-tuple-element.45), channel_id=1, source_target_pairs={{0,4},{1,5},{2,6},{3,7},{4,0},{5,1},{6,2},{7,3},{8,12},{9,13},{10,... | collective-permute-start | bytes 786440 | tf_op jit(solution)/shard_map/ppermute | solution.py:59
  43.4 17.4 %collective-permute-start.10 = (bf16[2,2,2,2,128,128]{5,4,3,2,1,0:T(8,128)(2,1)S(1)}, bf16[2,2,2,2,128,128]{5,4,3,2,1,0:T(8,128)(2,1)S(1)}, u32[]{:S(2)}, u32[]{:S(2)}) collective-permute-start(bf16[2,2,2,2,128,128]{5,4,3,2,1,0:T(8,128)(2,1)S(1)} %pad_maximum_fusion.1.refs_3_.refs_2_), channel_id=1, source_target_pairs={{0,32},{1,33},{2,34},{3,35},{4,12},{5,13},{6,14},{7,15},{8,40},{9,... | collective-permute-start | bytes 1572872 | tf_op jit(solution)/shard_map/ppermute | solution.py:59
  45.1 15.8 %collective-permute-start.11 = (bf16[2,2,2,2,128,128]{5,4,3,2,1,0:T(8,128)(2,1)S(1)}, bf16[2,2,2,2,128,128]{5,4,3,2,1,0:T(8,128)(2,1)S(1)}, u32[]{:S(2)}, u32[]{:S(2)}) collective-permute-start(bf16[2,2,2,2,128,128]{5,4,3,2,1,0:T(8,128)(2,1)S(1)} %pad_maximum_fusion.1.refs_3_.refs_2_), channel_id=1, source_target_pairs={{0,96},{1,97},{2,98},{3,99},{4,28},{5,29},{6,30},{7,31},{8,104},{9... | collective-permute-start | bytes 1572872 | tf_op jit(solution)/shard_map/ppermute | solution.py:59
  46.3 16.1 %collective-permute-start.12 = (bf16[2,2,2,2,128,128]{5,4,3,2,1,0:T(8,128)(2,1)S(1)}, bf16[2,2,2,2,128,128]{5,4,3,2,1,0:T(8,128)(2,1)S(1)}, u32[]{:S(2)}, u32[]{:S(2)}) collective-permute-start(bf16[2,2,2,2,128,128]{5,4,3,2,1,0:T(8,128)(2,1)S(1)} %pad_maximum_fusion.1.refs_3_.refs_2_), channel_id=1, source_target_pairs={{0,64},{1,65},{2,66},{3,67},{4,20},{5,21},{6,22},{7,23},{8,72},{9,... | collective-permute-start | bytes 1572872 | tf_op jit(solution)/shard_map/ppermute | solution.py:59
  67.5 13.9 %collective-permute-start.17 = (bf16[544,256]{1,0:T(8,128)(2,1)S(1)}, bf16[544,256]{1,0:T(8,128)(2,1)S(1)}, u32[]{:S(2)}, u32[]{:S(2)}) collective-permute-start(bf16[544,256]{1,0:T(8,128)(2,1)S(1)} %get-tuple-element.51), channel_id=1, source_target_pairs={{0,16},{1,17},{2,18},{3,19},{4,68},{5,69},{6,70},{7,71},{8,24},{9,... | collective-permute-start | bytes 835592 | tf_op jit(solution)/shard_map/ppermute | solution.py:59
  70.1 14.6 %collective-permute-start.18 = (bf16[544,256]{1,0:T(8,128)(2,1)S(1)}, bf16[544,256]{1,0:T(8,128)(2,1)S(1)}, u32[]{:S(2)}, u32[]{:S(2)}) collective-permute-start(bf16[544,256]{1,0:T(8,128)(2,1)S(1)} %get-tuple-element.52), channel_id=1, source_target_pairs={{0,24},{1,25},{2,26},{3,27},{4,100},{5,101},{6,102},{7,103},{8,0},... | collective-permute-start | bytes 835592 | tf_op jit(solution)/shard_map/ppermute | solution.py:59
  74.1 10.7 %collective-permute-start.19 = (bf16[544,256]{1,0:T(8,128)(2,1)S(1)}, bf16[544,256]{1,0:T(8,128)(2,1)S(1)}, u32[]{:S(2)}, u32[]{:S(2)}) collective-permute-start(bf16[544,256]{1,0:T(8,128)(2,1)S(1)} %get-tuple-element.53), channel_id=1, source_target_pairs={{0,8},{1,9},{2,10},{3,11},{4,36},{5,37},{6,38},{7,39},{8,16},{9,17... | collective-permute-start | bytes 835592 | tf_op jit(solution)/shard_map/ppermute | solution.py:59
  74.5 10.2 %collective-permute-start.20 = (bf16[544,256]{1,0:T(8,128)(2,1)S(1)}, bf16[544,256]{1,0:T(8,128)(2,1)S(1)}, u32[]{:S(2)}, u32[]{:S(2)}) collective-permute-start(bf16[544,256]{1,0:T(8,128)(2,1)S(1)} %get-tuple-element.55), channel_id=1, source_target_pairs={{0,20},{1,21},{2,22},{3,23},{4,64},{5,65},{6,66},{7,67},{8,28},{9,... | collective-permute-start | bytes 835592 | tf_op jit(solution)/shard_map/ppermute | solution.py:59
  77.0 8.0 %collective-permute-start.21 = (bf16[544,256]{1,0:T(8,128)(2,1)S(1)}, bf16[544,256]{1,0:T(8,128)(2,1)S(1)}, u32[]{:S(2)}, u32[]{:S(2)}) collective-permute-start(bf16[544,256]{1,0:T(8,128)(2,1)S(1)} %get-tuple-element.56), channel_id=1, source_target_pairs={{0,28},{1,29},{2,30},{3,31},{4,96},{5,97},{6,98},{7,99},{8,4},{9,5... | collective-permute-start | bytes 835592 | tf_op jit(solution)/shard_map/ppermute | solution.py:59
  81.4 7.5 %collective-permute-start.22 = (bf16[544,256]{1,0:T(8,128)(2,1)S(1)}, bf16[544,256]{1,0:T(8,128)(2,1)S(1)}, u32[]{:S(2)}, u32[]{:S(2)}) collective-permute-start(bf16[544,256]{1,0:T(8,128)(2,1)S(1)} %get-tuple-element.57), channel_id=1, source_target_pairs={{0,12},{1,13},{2,14},{3,15},{4,32},{5,33},{6,34},{7,35},{8,20},{9,... | collective-permute-start | bytes 835592 | tf_op jit(solution)/shard_map/ppermute | solution.py:59
  84.7 4.3 %collective-permute-start.23 = (bf16[544,256]{1,0:T(8,128)(2,1)S(1)}, bf16[544,256]{1,0:T(8,128)(2,1)S(1)}, u32[]{:S(2)}, u32[]{:S(2)}) collective-permute-start(bf16[544,256]{1,0:T(8,128)(2,1)S(1)} %get-tuple-element.58), channel_id=1, source_target_pairs={{0,4},{1,5},{2,6},{3,7},{4,0},{5,1},{6,2},{7,3},{8,12},{9,13},{10,... | collective-permute-start | bytes 835592 | tf_op jit(solution)/shard_map/ppermute | solution.py:59
  (5 other events, 52.0 us)

commit v4 on v3

--- a/solution.py
+++ b/solution.py
@@ -229,6 +229,8 @@
     ones = jnp.where(row == col, 1.0, 0.0).astype(BF16)
     empty = jnp.zeros((HD, BLOCK), BF16)
 
+    encoders = [dp_index(core == 0, offset, swapped) for offset in OFFSETS for swapped in range(2)]
+
     def question(index, carry):
         number = index >> 1
         offset, offset_slot = jnp.int32(OFFSETS[slots[0]]), jnp.int32(slots[0])
@@ -239,15 +241,19 @@
         count = jnp.int32(0)
         for t in range(4):
             for swapped in range(2):
-                local = wanted[q_index, dp_index(core == 0, OFFSETS[t], swapped)]
+                local = wanted[q_index, encoders[2 * t + swapped]]
                 chosen[count] = (t * 2 + swapped) * 2 + jnp.maximum(local, 0)
                 count = count + jnp.where(local >= 0, 1, 0)
         for pair in range(PART):
             query = qbuf[index, :, pair * TILE : (pair + 1) * TILE]
             for head in range(2):
                 masked[pair, head] = jnp.where(lane_half == head, query, jnp.zeros_like(query))
-        run_sums[...] = jnp.zeros((PART, SUMS, QTOK), F32)
-        run_tops[...] = jnp.full((8, QTOK), LOW, F32)
+
+        @pl.when(count == 0)
+        def _():
+            run_sums[...] = jnp.zeros((PART, SUMS, QTOK), F32)
+            run_tops[...] = jnp.full((8, QTOK), LOW, F32)
+
         chosen[count] = chosen[jnp.maximum(count - 1, 0)]
 
         def weigh(size):
@@ -452,7 +458,7 @@
     slots_q = [q_pair, q_left, q_right, q_far]
     early = attend(0, wanted, slots_q, kv, (0, 1, 2, 3))
     mine, away = [], []
-    for slots in ((3, 1), (2,), (0,)):
+    for slots in ((3,), (1, 2), (0,)):
         outs = attend(1, wanted, slots_q, kv_late, slots, early)
         for number, slot in enumerate(slots):
             same, cross = outs[2 * number : 2 * number + 2]

time: 91 us -> 91.4 us (level)
  waiting for transfers between devices: 13.3 us -> 14.6 us
    ppermute x24, waiting for transfers between devices: 13.3 us -> 14.6 us  [send(): return lax.ppermute(array, AXES, pairs)]
  transfers between devices with their start and end apart: 24 -> 24, of which waited for: 7 -> 7; matrix products, arithmetic and copies ran while one was open for 1% -> 1% of each run, Pallas kernels for 25% -> 27%
where the time goes in v4:
time: 91.4 us; the launch traced here: 90.8 us
  starting transfers between devices  39.5 us (43%)
  Pallas kernels  28.5 us (31%)
  waiting for transfers between devices  14.6 us (16%)
  local copies, waits for them, and re-layouts  7.82 us (9%)
    ppermute x24, starting transfers between devices, send(): return lax.ppermute(array, AXES, pairs)  39.5 us
    pallas_call x4, Pallas kernels, attend(): pl.pallas_call(functools.partial(attend_kernel, part, slots), out_shape=o...  20 us
    ppermute x24, waiting for transfers between devices, send(): return lax.ppermute(array, AXES, pairs)  14.6 us
    unnamed x10, local copies, waits for them, and re-layouts  6.78 us
    pallas_call x2, Pallas kernels, project(): pl.pallas_call(functools.partial(project_kernel, part), out_shape=tuple(s...  5.86 us
  transfers between devices with their start and end apart: 24, of which 7 were waited for; matrix products, arithmetic and copies ran while one was open for 1% of the time, Pallas kernels for 27%

profile of v4, /device:TPU:1, one launch (start us, length us, event | category | flops | bytes accessed | tf_op | source)
XLA Modules:
  0.0 90.8 jit_solution(17461169553719436580)
XLA Ops:
  5.3 2.8 %collective-permute-start.1 = (bf16[2,256,512]{2,1,0:T(8,128)(2,1)S(1)}, bf16[2,256,512]{2,1,0:T(8,128)(2,1)S(1)}, u32[]{:S(2)}, u32[]{:S(2)}) collective-permute-start(bf16[2,256,512]{2,1,0:T(8,128)(2,1)S(1)} %pad_maximum_fusion.refs_1_), channel_id=1, source_target_pairs={{0,16},{1,17},{2,18},{3,19},{4,68},{5,69},{6,70},{7,71},{8,24},{9,... | collective-permute-start | bytes 1572872 | tf_op jit(solution)/shard_map/ppermute | solution.py:59
  9.0 3.4 %copy-done = bf16[4096,1024]{1,0:T(8,128)(2,1)S(1)} copy-done((bf16[4096,1024]{1,0:T(8,128)(2,1)S(1)}, bf16[4096,1024]{1,0:T(8,128)(2,1)}, u32[]{:S(2)}) %copy-start) | copy-done | bytes 8388632
  12.4 3.4 %copy-done.1 = bf16[4096,1024]{1,0:T(8,128)(2,1)S(1)} copy-done((bf16[4096,1024]{1,0:T(8,128)(2,1)S(1)}, bf16[4096,1024]{1,0:T(8,128)(2,1)}, u32[]{:S(2)}) %copy-start.1) | copy-done | bytes 8388632
  17.7 2.1 %collective-permute-start.6 = (bf16[144,1024]{1,0:T(8,128)(2,1)S(1)}, bf16[144,1024]{1,0:T(8,128)(2,1)S(1)}, u32[]{:S(2)}, u32[]{:S(2)}) collective-permute-start(bf16[144,1024]{1,0:T(8,128)(2,1)S(1)} %get-tuple-element.59), channel_id=1, source_target_pairs={{0,3},{1,0},{2,1},{3,2},{4,7},{5,4},{6,5},{7,6},{8,11},{9,8},{10,9... | collective-permute-start | bytes 884744 | tf_op jit(solution)/shard_map/ppermute | solution.py:59
  20.5 4.8 %collective-permute-done.5.refs_3_ = bf16[144,1024]{1,0:T(8,128)(2,1)S(1)} collective-permute-done((bf16[144,1024]{1,0:T(8,128)(2,1)S(1)}, bf16[144,1024]{1,0:T(8,128)(2,1)S(1)}, u32[]{:S(2)}, u32[]{:S(2)}) %collective-permute-start.5) | collective-permute-done | bytes 294944 | tf_op jit(solution)/shard_map/ppermute | solution.py:59
  26.3 3.4 %project.2 = (bf16[2,2,2,128,128]{4,3,2,1,0:T(8,128)(2,1)S(1)}, bf16[2,2,2,128,128]{4,3,2,1,0:T(8,128)(2,1)S(1)}, bf16[4,256,1024]{2,1,0:T(8,128)(2,1)S(1)}) custom-call(bf16[256,1024]{1,0:T(8,128)(2,1)S(1)} %bitcast.11, bf16[256,1024]{1,0:T(8,128)(2,1)S(1)} %collective-permute-done.3.refs_1_, bf16[256,1024]{1,0:T(8,128)(2,1)S(1)} %collective-permute-done.4.refs_2_, ...), custom_call_target="tpu_custom_call" | custom-call | bytes 1024 | tf_op jit(solution)/shard_map/project/pallas_call | solution.py:162
  29.6 3.6 %collective-permute-start.13 = (bf16[2,2,2,128,128]{4,3,2,1,0:T(8,128)(2,1)S(1)}, bf16[2,2,2,128,128]{4,3,2,1,0:T(8,128)(2,1)S(1)}, u32[]{:S(2)}, u32[]{:S(2)}) collective-permute-start(bf16[2,2,2,128,128]{4,3,2,1,0:T(8,128)(2,1)S(1)} %get-tuple-element.48), channel_id=1, source_target_pairs={{0,4},{1,5},{2,6},{3,7},{4,0},{5,1},{6,2},{7,3},{8,12},{9,13},{10,... | collective-permute-start | bytes 786440 | tf_op jit(solution)/shard_map/ppermute | solution.py:59
  34.4 1.7 %collective-permute-start.14 = (bf16[2,2,2,2,128,128]{5,4,3,2,1,0:T(8,128)(2,1)S(1)}, bf16[2,2,2,2,128,128]{5,4,3,2,1,0:T(8,128)(2,1)S(1)}, u32[]{:S(2)}, u32[]{:S(2)}) collective-permute-start(bf16[2,2,2,2,128,128]{5,4,3,2,1,0:T(8,128)(2,1)S(1)} %pad_maximum_fusion.2.refs_5_), channel_id=1, source_target_pairs={{0,32},{1,33},{2,34},{3,35},{4,12},{5,13},{6,14},{7,15},{8,40},{9,... | collective-permute-start | bytes 1572872 | tf_op jit(solution)/shard_map/ppermute | solution.py:59
  37.2 2.1 %collective-permute-start.16 = (bf16[2,2,2,2,128,128]{5,4,3,2,1,0:T(8,128)(2,1)S(1)}, bf16[2,2,2,2,128,128]{5,4,3,2,1,0:T(8,128)(2,1)S(1)}, u32[]{:S(2)}, u32[]{:S(2)}) collective-permute-start(bf16[2,2,2,2,128,128]{5,4,3,2,1,0:T(8,128)(2,1)S(1)} %pad_maximum_fusion.2.refs_5_), channel_id=1, source_target_pairs={{0,64},{1,65},{2,66},{3,67},{4,20},{5,21},{6,22},{7,23},{8,72},{9,... | collective-permute-start | bytes 1572872 | tf_op jit(solution)/shard_map/ppermute | solution.py:59
  39.3 2.5 %project.3 = (bf16[2,2,2,128,128]{4,3,2,1,0:T(8,128)(2,1)S(1)}, bf16[2,2,2,128,128]{4,3,2,1,0:T(8,128)(2,1)S(1)}) custom-call(bf16[4,256,1024]{2,1,0:T(8,128)(2,1)S(1)} %get-tuple-element.42.refs_0_, bf16[4096,1024]{1,0:T(8,128)(2,1)S(1)} %get-tuple-element.38.refs_7_.refs_1_, bf16[4096,1024]{1,0:T(8,128)(2,1)S(1)} %get-tuple-element.39.refs_8_.refs_2_), custom_call_target="tpu_custom_call" | custom-call | bytes 1024 | tf_op jit(solution)/shard_map/project/pallas_call | solution.py:162
  43.4 1.7 %collective-permute-start.10 = (bf16[2,2,2,2,128,128]{5,4,3,2,1,0:T(8,128)(2,1)S(1)}, bf16[2,2,2,2,128,128]{5,4,3,2,1,0:T(8,128)(2,1)S(1)}, u32[]{:S(2)}, u32[]{:S(2)}) collective-permute-start(bf16[2,2,2,2,128,128]{5,4,3,2,1,0:T(8,128)(2,1)S(1)} %pad_maximum_fusion.1.refs_2_.refs_3_), channel_id=1, source_target_pairs={{0,32},{1,33},{2,34},{3,35},{4,12},{5,13},{6,14},{7,15},{8,40},{9,... | collective-permute-start | bytes 1572872 | tf_op jit(solution)/shard_map/ppermute | solution.py:59
  46.3 5.5 %collective-permute-start.12 = (bf16[2,2,2,2,128,128]{5,4,3,2,1,0:T(8,128)(2,1)S(1)}, bf16[2,2,2,2,128,128]{5,4,3,2,1,0:T(8,128)(2,1)S(1)}, u32[]{:S(2)}, u32[]{:S(2)}) collective-permute-start(bf16[2,2,2,2,128,128]{5,4,3,2,1,0:T(8,128)(2,1)S(1)} %pad_maximum_fusion.1.refs_2_.refs_3_), channel_id=1, source_target_pairs={{0,64},{1,65},{2,66},{3,67},{4,20},{5,21},{6,22},{7,23},{8,72},{9,... | collective-permute-start | bytes 1572872 | tf_op jit(solution)/shard_map/ppermute | solution.py:59
  51.8 8.9 %attend.4 = (bf16[8,256,256]{2,1,0:T(8,128)(2,1)S(1)}, f32[8,8,256]{2,1,0:T(8,128)S(1)}) custom-call(s32[32,32]{1,0:T(8,128)S(1)} %copy-done.4, bf16[2,256,512]{2,1,0:T(8,128)(2,1)S(1)} %pad_maximum_fusion.refs_1_, bf16[2,256,512]{2,1,0:T(8,128)(2,1)S(1)} %collective-permute-done.8.refs_2_.refs_1_, ...), custom_call_target="tpu_custom_call" | custom-call | flops 8000000000 | bytes 8388608 | tf_op jit(solution)/shard_map/attend/pallas_call | solution.py:355
  60.7 1.7 %collective-permute-done.12.refs_5_.refs_6_ = bf16[2,2,2,2,128,128]{5,4,3,2,1,0:T(8,128)(2,1)S(1)} collective-permute-done((bf16[2,2,2,2,128,128]{5,4,3,2,1,0:T(8,128)(2,1)S(1)}, bf16[2,2,2,2,128,128]{5,4,3,2,1,0:T(8,128)(2,1)S(1)}, u32[]{:S(2)}, u32[]{:S(2)}) %collective-permute-start.12) | collective-permute-done | bytes 524320 | tf_op jit(solution)/shard_map/ppermute | solution.py:59
  62.4 2.7 %attend.5 = (bf16[544,256]{1,0:T(8,128)(2,1)S(1)}, bf16[544,256]{1,0:T(8,128)(2,1)S(1)}) custom-call(s32[32,32]{1,0:T(8,128)S(1)} %copy-done.4, bf16[2,256,512]{2,1,0:T(8,128)(2,1)S(1)} %collective-permute-done.1.refs_4_.refs_1_, bf16[2,2,2,2,128,128]{5,4,3,2,1,0:T(8,128)(2,1)S(1)} %pad_maximum_fusion.1.refs_2_.refs_3_, ...), custom_call_target="tpu_custom_call" | custom-call | flops 2000000000 | bytes 8388608 | tf_op jit(solution)/shard_map/attend/pallas_call | solution.py:355
  65.1 2.6 %collective-permute-start.17 = (bf16[544,256]{1,0:T(8,128)(2,1)S(1)}, bf16[544,256]{1,0:T(8,128)(2,1)S(1)}, u32[]{:S(2)}, u32[]{:S(2)}) collective-permute-start(bf16[544,256]{1,0:T(8,128)(2,1)S(1)} %get-tuple-element.51), channel_id=1, source_target_pairs={{0,16},{1,17},{2,18},{3,19},{4,68},{5,69},{6,70},{7,71},{8,24},{9,... | collective-permute-start | bytes 835592 | tf_op jit(solution)/shard_map/ppermute | solution.py:59
  67.7 5.1 %attend.6 = (bf16[544,256]{1,0:T(8,128)(2,1)S(1)}, bf16[544,256]{1,0:T(8,128)(2,1)S(1)}, bf16[544,256]{1,0:T(8,128)(2,1)S(1)}, bf16[544,256]{1,0:T(8,128)(2,1)S(1)}) custom-call(s32[32,32]{1,0:T(8,128)S(1)} %copy-done.4, bf16[2,256,512]{2,1,0:T(8,128)(2,1)S(1)} %collective-permute-done.8.refs_2_.refs_1_, ...), custom_call_target="tpu_custom_call" | custom-call | flops 4000000000 | bytes 8388608 | tf_op jit(solution)/shard_map/attend/pallas_call | solution.py:355
  74.3 2.4 %collective-permute-start.20 = (bf16[544,256]{1,0:T(8,128)(2,1)S(1)}, bf16[544,256]{1,0:T(8,128)(2,1)S(1)}, u32[]{:S(2)}, u32[]{:S(2)}) collective-permute-start(bf16[544,256]{1,0:T(8,128)(2,1)S(1)} %get-tuple-element.55), channel_id=1, source_target_pairs={{0,20},{1,21},{2,22},{3,23},{4,64},{5,65},{6,66},{7,67},{8,28},{9,... | collective-permute-start | bytes 835592 | tf_op jit(solution)/shard_map/ppermute | solution.py:59
  76.8 1.8 %collective-permute-start.21 = (bf16[544,256]{1,0:T(8,128)(2,1)S(1)}, bf16[544,256]{1,0:T(8,128)(2,1)S(1)}, u32[]{:S(2)}, u32[]{:S(2)}) collective-permute-start(bf16[544,256]{1,0:T(8,128)(2,1)S(1)} %get-tuple-element.56), channel_id=1, source_target_pairs={{0,28},{1,29},{2,30},{3,31},{4,96},{5,97},{6,98},{7,99},{8,4},{9,5... | collective-permute-start | bytes 835592 | tf_op jit(solution)/shard_map/ppermute | solution.py:59
  78.5 3.4 %attend.7 = (bf16[544,256]{1,0:T(8,128)(2,1)S(1)}, bf16[544,256]{1,0:T(8,128)(2,1)S(1)}) custom-call(s32[32,32]{1,0:T(8,128)S(1)} %copy-done.4, bf16[2,256,512]{2,1,0:T(8,128)(2,1)S(1)} %pad_maximum_fusion.refs_1_, bf16[2,2,2,2,128,128]{5,4,3,2,1,0:T(8,128)(2,1)S(1)} %pad_maximum_fusion.1.refs_2_.refs_3_, ...), custom_call_target="tpu_custom_call" | custom-call | flops 2000000000 | bytes 8388608 | tf_op jit(solution)/shard_map/attend/pallas_call | solution.py:355
  81.9 2.2 %collective-permute-start.22 = (bf16[544,256]{1,0:T(8,128)(2,1)S(1)}, bf16[544,256]{1,0:T(8,128)(2,1)S(1)}, u32[]{:S(2)}, u32[]{:S(2)}) collective-permute-start(bf16[544,256]{1,0:T(8,128)(2,1)S(1)} %get-tuple-element.57), channel_id=1, source_target_pairs={{0,12},{1,13},{2,14},{3,15},{4,32},{5,33},{6,34},{7,35},{8,20},{9,... | collective-permute-start | bytes 835592 | tf_op jit(solution)/shard_map/ppermute | solution.py:59
  84.1 2.4 %collective-permute-done.21.refs_5_ = bf16[544,256]{1,0:T(8,128)(2,1)S(1)} collective-permute-done((bf16[544,256]{1,0:T(8,128)(2,1)S(1)}, bf16[544,256]{1,0:T(8,128)(2,1)S(1)}, u32[]{:S(2)}, u32[]{:S(2)}) %collective-permute-start.21) | collective-permute-done | bytes 278560 | tf_op jit(solution)/shard_map/ppermute | solution.py:59
  86.5 2.8 %collective-permute-done.22.refs_6_ = bf16[544,256]{1,0:T(8,128)(2,1)S(1)} collective-permute-done((bf16[544,256]{1,0:T(8,128)(2,1)S(1)}, bf16[544,256]{1,0:T(8,128)(2,1)S(1)}, u32[]{:S(2)}, u32[]{:S(2)}) %collective-permute-start.22) | collective-permute-done | bytes 278560 | tf_op jit(solution)/shard_map/ppermute | solution.py:59
  89.3 1.5 %merge.1 = bf16[256,1024]{1,0:T(8,128)(2,1)} custom-call(bf16[544,256]{1,0:T(8,128)(2,1)S(1)} %collective-permute-done.17.refs_0_, bf16[544,256]{1,0:T(8,128)(2,1)S(1)} %collective-permute-done.18.refs_1_, bf16[544,256]{1,0:T(8,128)(2,1)S(1)} %collective-permute-done.19.refs_2_, bf16[544,256]{1,0:T(8,128)(2,1)S(1)} %get-tuple-element.54.refs_3_, ...), custom_call_target="tpu_custom_call" | custom-call | tf_op jit(solution)/shard_map/merge/pallas_call | solution.py:417
  (51 shorter events, 16.3 us)
Async XLA Ops:
  0.0 5.2 %collective-permute-start = (bf16[256,1024]{1,0:T(8,128)(2,1)}, bf16[256,1024]{1,0:T(8,128)(2,1)S(1)}, u32[]{:S(2)}, u32[]{:S(2)}) collective-permute-start(bf16[256,1024]{1,0:T(8,128)(2,1)} %param.10), channel_id=1, source_target_pairs={{0,4},{1,5},{2,6},{3,7},{4,0},{5,1},{6,2},{7,3},{8,12},{9,13},{10,... | collective-permute-start | bytes 1572872 | tf_op jit(solution)/shard_map/ppermute | solution.py:59
  1.4 15.5 %collective-permute-start.3 = (bf16[256,1024]{1,0:T(8,128)(2,1)}, bf16[256,1024]{1,0:T(8,128)(2,1)S(1)}, u32[]{:S(2)}, u32[]{:S(2)}) collective-permute-start(bf16[256,1024]{1,0:T(8,128)(2,1)} %bitcast.9), channel_id=1, source_target_pairs={{0,1},{1,2},{2,3},{3,0},{4,5},{5,6},{6,7},{7,4},{8,9},{9,10},{10,1... | collective-permute-start | bytes 1572872 | tf_op jit(solution)/shard_map/ppermute | solution.py:59
  2.8 14.1 %collective-permute-start.4 = (bf16[256,1024]{1,0:T(8,128)(2,1)}, bf16[256,1024]{1,0:T(8,128)(2,1)S(1)}, u32[]{:S(2)}, u32[]{:S(2)}) collective-permute-start(bf16[256,1024]{1,0:T(8,128)(2,1)} %bitcast.10), channel_id=1, source_target_pairs={{0,3},{1,0},{2,1},{3,2},{4,7},{5,4},{6,5},{7,6},{8,11},{9,8},{10,9... | collective-permute-start | bytes 1572872 | tf_op jit(solution)/shard_map/ppermute | solution.py:59
  5.3 20.6 %collective-permute-start.1 = (bf16[2,256,512]{2,1,0:T(8,128)(2,1)S(1)}, bf16[2,256,512]{2,1,0:T(8,128)(2,1)S(1)}, u32[]{:S(2)}, u32[]{:S(2)}) collective-permute-start(bf16[2,256,512]{2,1,0:T(8,128)(2,1)S(1)} %pad_maximum_fusion.refs_1_), channel_id=1, source_target_pairs={{0,16},{1,17},{2,18},{3,19},{4,68},{5,69},{6,70},{7,71},{8,24},{9,... | collective-permute-start | bytes 1572872 | tf_op jit(solution)/shard_map/ppermute | solution.py:59
  8.2 17.7 %collective-permute-start.2 = (bf16[2,256,512]{2,1,0:T(8,128)(2,1)S(1)}, bf16[2,256,512]{2,1,0:T(8,128)(2,1)S(1)}, u32[]{:S(2)}, u32[]{:S(2)}) collective-permute-start(bf16[2,256,512]{2,1,0:T(8,128)(2,1)S(1)} %pad_maximum_fusion.refs_1_), channel_id=1, source_target_pairs={{0,24},{1,25},{2,26},{3,27},{4,100},{5,101},{6,102},{7,103},{8,0},... | collective-permute-start | bytes 1572872 | tf_op jit(solution)/shard_map/ppermute | solution.py:59
  17.1 8.3 %collective-permute-start.5 = (bf16[144,1024]{1,0:T(8,128)(2,1)S(1)}, bf16[144,1024]{1,0:T(8,128)(2,1)S(1)}, u32[]{:S(2)}, u32[]{:S(2)}) collective-permute-start(bf16[144,1024]{1,0:T(8,128)(2,1)S(1)} %get-tuple-element.60), channel_id=1, source_target_pairs={{0,1},{1,2},{2,3},{3,0},{4,5},{5,6},{6,7},{7,4},{8,9},{9,10},{10,1... | collective-permute-start | bytes 884744 | tf_op jit(solution)/shard_map/ppermute | solution.py:59
  17.7 8.5 %collective-permute-start.6 = (bf16[144,1024]{1,0:T(8,128)(2,1)S(1)}, bf16[144,1024]{1,0:T(8,128)(2,1)S(1)}, u32[]{:S(2)}, u32[]{:S(2)}) collective-permute-start(bf16[144,1024]{1,0:T(8,128)(2,1)S(1)} %get-tuple-element.59), channel_id=1, source_target_pairs={{0,3},{1,0},{2,1},{3,2},{4,7},{5,4},{6,5},{7,6},{8,11},{9,8},{10,9... | collective-permute-start | bytes 884744 | tf_op jit(solution)/shard_map/ppermute | solution.py:59
  19.8 6.4 %collective-permute-start.7 = (bf16[1024]{0:T(1024)(128)(2,1)S(1)}, bf16[1024]{0:T(1024)(128)(2,1)S(1)}, u32[]{:S(2)}, u32[]{:S(2)}) collective-permute-start(bf16[1024]{0:T(1024)(128)(2,1)S(1)} %copy-done.3), channel_id=1, source_target_pairs={{0,2},{1,3},{2,0},{3,1},{4,6},{5,7},{6,4},{7,5},{8,10},{9,11},{10,... | collective-permute-start | bytes 6152 | tf_op jit(solution)/shard_map/ppermute | solution.py:59
  25.4 13.9 %collective-permute-start.8 = (bf16[2,256,512]{2,1,0:T(8,128)(2,1)S(1)}, bf16[2,256,512]{2,1,0:T(8,128)(2,1)S(1)}, u32[]{:S(2)}, u32[]{:S(2)}) collective-permute-start(bf16[2,256,512]{2,1,0:T(8,128)(2,1)S(1)} %pad_maximum_fusion.refs_1_), channel_id=1, source_target_pairs={{0,8},{1,9},{2,10},{3,11},{4,36},{5,37},{6,38},{7,39},{8,16},{9,17... | collective-permute-start | bytes 1572872 | tf_op jit(solution)/shard_map/ppermute | solution.py:59
  29.6 4.7 %collective-permute-start.13 = (bf16[2,2,2,128,128]{4,3,2,1,0:T(8,128)(2,1)S(1)}, bf16[2,2,2,128,128]{4,3,2,1,0:T(8,128)(2,1)S(1)}, u32[]{:S(2)}, u32[]{:S(2)}) collective-permute-start(bf16[2,2,2,128,128]{4,3,2,1,0:T(8,128)(2,1)S(1)} %get-tuple-element.48), channel_id=1, source_target_pairs={{0,4},{1,5},{2,6},{3,7},{4,0},{5,1},{6,2},{7,3},{8,12},{9,13},{10,... | collective-permute-start | bytes 786440 | tf_op jit(solution)/shard_map/ppermute | solution.py:59
  34.4 11.8 %collective-permute-start.14 = (bf16[2,2,2,2,128,128]{5,4,3,2,1,0:T(8,128)(2,1)S(1)}, bf16[2,2,2,2,128,128]{5,4,3,2,1,0:T(8,128)(2,1)S(1)}, u32[]{:S(2)}, u32[]{:S(2)}) collective-permute-start(bf16[2,2,2,2,128,128]{5,4,3,2,1,0:T(8,128)(2,1)S(1)} %pad_maximum_fusion.2.refs_5_), channel_id=1, source_target_pairs={{0,32},{1,33},{2,34},{3,35},{4,12},{5,13},{6,14},{7,15},{8,40},{9,... | collective-permute-start | bytes 1572872 | tf_op jit(solution)/shard_map/ppermute | solution.py:59
  36.1 15.6 %collective-permute-start.15 = (bf16[2,2,2,2,128,128]{5,4,3,2,1,0:T(8,128)(2,1)S(1)}, bf16[2,2,2,2,128,128]{5,4,3,2,1,0:T(8,128)(2,1)S(1)}, u32[]{:S(2)}, u32[]{:S(2)}) collective-permute-start(bf16[2,2,2,2,128,128]{5,4,3,2,1,0:T(8,128)(2,1)S(1)} %pad_maximum_fusion.2.refs_5_), channel_id=1, source_target_pairs={{0,96},{1,97},{2,98},{3,99},{4,28},{5,29},{6,30},{7,31},{8,104},{9... | collective-permute-start | bytes 1572872 | tf_op jit(solution)/shard_map/ppermute | solution.py:59
  37.2 14.6 %collective-permute-start.16 = (bf16[2,2,2,2,128,128]{5,4,3,2,1,0:T(8,128)(2,1)S(1)}, bf16[2,2,2,2,128,128]{5,4,3,2,1,0:T(8,128)(2,1)S(1)}, u32[]{:S(2)}, u32[]{:S(2)}) collective-permute-start(bf16[2,2,2,2,128,128]{5,4,3,2,1,0:T(8,128)(2,1)S(1)} %pad_maximum_fusion.2.refs_5_), channel_id=1, source_target_pairs={{0,64},{1,65},{2,66},{3,67},{4,20},{5,21},{6,22},{7,23},{8,72},{9,... | collective-permute-start | bytes 1572872 | tf_op jit(solution)/shard_map/ppermute | solution.py:59
  41.8 1.6 %collective-permute-start.9 = (bf16[2,2,2,128,128]{4,3,2,1,0:T(8,128)(2,1)S(1)}, bf16[2,2,2,128,128]{4,3,2,1,0:T(8,128)(2,1)S(1)}, u32[]{:S(2)}, u32[]{:S(2)}) collective-permute-start(bf16[2,2,2,128,128]{4,3,2,1,0:T(8,128)(2,1)S(1)} %get-tuple-element.44), channel_id=1, source_target_pairs={{0,4},{1,5},{2,6},{3,7},{4,0},{5,1},{6,2},{7,3},{8,12},{9,13},{10,... | collective-permute-start | bytes 786440 | tf_op jit(solution)/shard_map/ppermute | solution.py:59
  43.4 17.2 %collective-permute-start.10 = (bf16[2,2,2,2,128,128]{5,4,3,2,1,0:T(8,128)(2,1)S(1)}, bf16[2,2,2,2,128,128]{5,4,3,2,1,0:T(8,128)(2,1)S(1)}, u32[]{:S(2)}, u32[]{:S(2)}) collective-permute-start(bf16[2,2,2,2,128,128]{5,4,3,2,1,0:T(8,128)(2,1)S(1)} %pad_maximum_fusion.1.refs_2_.refs_3_), channel_id=1, source_target_pairs={{0,32},{1,33},{2,34},{3,35},{4,12},{5,13},{6,14},{7,15},{8,40},{9,... | collective-permute-start | bytes 1572872 | tf_op jit(solution)/shard_map/ppermute | solution.py:59
  45.1 15.6 %collective-permute-start.11 = (bf16[2,2,2,2,128,128]{5,4,3,2,1,0:T(8,128)(2,1)S(1)}, bf16[2,2,2,2,128,128]{5,4,3,2,1,0:T(8,128)(2,1)S(1)}, u32[]{:S(2)}, u32[]{:S(2)}) collective-permute-start(bf16[2,2,2,2,128,128]{5,4,3,2,1,0:T(8,128)(2,1)S(1)} %pad_maximum_fusion.1.refs_2_.refs_3_), channel_id=1, source_target_pairs={{0,96},{1,97},{2,98},{3,99},{4,28},{5,29},{6,30},{7,31},{8,104},{9... | collective-permute-start | bytes 1572872 | tf_op jit(solution)/shard_map/ppermute | solution.py:59
  46.3 16.1 %collective-permute-start.12 = (bf16[2,2,2,2,128,128]{5,4,3,2,1,0:T(8,128)(2,1)S(1)}, bf16[2,2,2,2,128,128]{5,4,3,2,1,0:T(8,128)(2,1)S(1)}, u32[]{:S(2)}, u32[]{:S(2)}) collective-permute-start(bf16[2,2,2,2,128,128]{5,4,3,2,1,0:T(8,128)(2,1)S(1)} %pad_maximum_fusion.1.refs_2_.refs_3_), channel_id=1, source_target_pairs={{0,64},{1,65},{2,66},{3,67},{4,20},{5,21},{6,22},{7,23},{8,72},{9,... | collective-permute-start | bytes 1572872 | tf_op jit(solution)/shard_map/ppermute | solution.py:59
  65.1 16.8 %collective-permute-start.17 = (bf16[544,256]{1,0:T(8,128)(2,1)S(1)}, bf16[544,256]{1,0:T(8,128)(2,1)S(1)}, u32[]{:S(2)}, u32[]{:S(2)}) collective-permute-start(bf16[544,256]{1,0:T(8,128)(2,1)S(1)} %get-tuple-element.51), channel_id=1, source_target_pairs={{0,16},{1,17},{2,18},{3,19},{4,68},{5,69},{6,70},{7,71},{8,24},{9,... | collective-permute-start | bytes 835592 | tf_op jit(solution)/shard_map/ppermute | solution.py:59
  72.8 11.3 %collective-permute-start.18 = (bf16[544,256]{1,0:T(8,128)(2,1)S(1)}, bf16[544,256]{1,0:T(8,128)(2,1)S(1)}, u32[]{:S(2)}, u32[]{:S(2)}) collective-permute-start(bf16[544,256]{1,0:T(8,128)(2,1)S(1)} %get-tuple-element.52), channel_id=1, source_target_pairs={{0,24},{1,25},{2,26},{3,27},{4,100},{5,101},{6,102},{7,103},{8,0},... | collective-permute-start | bytes 835592 | tf_op jit(solution)/shard_map/ppermute | solution.py:59
  73.1 11.0 %collective-permute-start.19 = (bf16[544,256]{1,0:T(8,128)(2,1)S(1)}, bf16[544,256]{1,0:T(8,128)(2,1)S(1)}, u32[]{:S(2)}, u32[]{:S(2)}) collective-permute-start(bf16[544,256]{1,0:T(8,128)(2,1)S(1)} %get-tuple-element.53), channel_id=1, source_target_pairs={{0,8},{1,9},{2,10},{3,11},{4,36},{5,37},{6,38},{7,39},{8,16},{9,17... | collective-permute-start | bytes 835592 | tf_op jit(solution)/shard_map/ppermute | solution.py:59
  74.3 9.8 %collective-permute-start.20 = (bf16[544,256]{1,0:T(8,128)(2,1)S(1)}, bf16[544,256]{1,0:T(8,128)(2,1)S(1)}, u32[]{:S(2)}, u32[]{:S(2)}) collective-permute-start(bf16[544,256]{1,0:T(8,128)(2,1)S(1)} %get-tuple-element.55), channel_id=1, source_target_pairs={{0,20},{1,21},{2,22},{3,23},{4,64},{5,65},{6,66},{7,67},{8,28},{9,... | collective-permute-start | bytes 835592 | tf_op jit(solution)/shard_map/ppermute | solution.py:59
  76.8 9.7 %collective-permute-start.21 = (bf16[544,256]{1,0:T(8,128)(2,1)S(1)}, bf16[544,256]{1,0:T(8,128)(2,1)S(1)}, u32[]{:S(2)}, u32[]{:S(2)}) collective-permute-start(bf16[544,256]{1,0:T(8,128)(2,1)S(1)} %get-tuple-element.56), channel_id=1, source_target_pairs={{0,28},{1,29},{2,30},{3,31},{4,96},{5,97},{6,98},{7,99},{8,4},{9,5... | collective-permute-start | bytes 835592 | tf_op jit(solution)/shard_map/ppermute | solution.py:59
  81.9 7.4 %collective-permute-start.22 = (bf16[544,256]{1,0:T(8,128)(2,1)S(1)}, bf16[544,256]{1,0:T(8,128)(2,1)S(1)}, u32[]{:S(2)}, u32[]{:S(2)}) collective-permute-start(bf16[544,256]{1,0:T(8,128)(2,1)S(1)} %get-tuple-element.57), channel_id=1, source_target_pairs={{0,12},{1,13},{2,14},{3,15},{4,32},{5,33},{6,34},{7,35},{8,20},{9,... | collective-permute-start | bytes 835592 | tf_op jit(solution)/shard_map/ppermute | solution.py:59
  84.1 5.2 %collective-permute-start.23 = (bf16[544,256]{1,0:T(8,128)(2,1)S(1)}, bf16[544,256]{1,0:T(8,128)(2,1)S(1)}, u32[]{:S(2)}, u32[]{:S(2)}) collective-permute-start(bf16[544,256]{1,0:T(8,128)(2,1)S(1)} %get-tuple-element.58), channel_id=1, source_target_pairs={{0,4},{1,5},{2,6},{3,7},{4,0},{5,1},{6,2},{7,3},{8,12},{9,13},{10,... | collective-permute-start | bytes 835592 | tf_op jit(solution)/shard_map/ppermute | solution.py:59
  (5 other events, 52.0 us)
